TPU v7x, 128 devices: a whole 4x4x4 slice. The times are simulated.
128 devices in a mesh: blk: 32 (over x, z, y_lo), rep: 4 (over y_hi, core).
Axes of the slice: x: 4, y: 4 (y_hi: 2, y_lo: 2; y = y_hi * 2 + y_lo), z: 4, core: 2. Of those that a mesh axis runs over, the one named last changes fastest.
Arguments:
- points: float32 [32, 32768], P(None, 'blk'), may hold values from -6 to 6
- lengthscale: float32 [32], replicated, may hold values from 1.5 to 6
- noise: float32 [1], replicated, may hold values from 0.5 to 2
- solution: float32 [16, 32768], P('rep', 'blk'), may hold values from -6 to 6
- residual: float32 [16, 32768], P('rep', 'blk'), may hold values from -11 to 11
- direction: float32 [16, 32768], P('rep', 'blk'), may hold values from -6 to 6
Outputs:
- new_solution: float32 [16, 32768], P('rep', 'blk')
- new_residual: float32 [16, 32768], P('rep', 'blk')
- new_direction: float32 [16, 32768], P('rep', 'blk')
All inputs are finite; a program needn't handle non-finite values.
Results may differ from a plain program's by a relative error of at most 0.035.
Values may be sent and summed in bfloat16 or wider, within the bound.
A program may use at most 64 MiB of HBM per device.

v0:
```python
import math

import jax
import jax.numpy as jnp
from jax import lax
from jax.sharding import PartitionSpec as P

root_five = math.sqrt(5.0)


def kernel_tile(scaled, sq_norms, col_pts, col_sq):
    cross = lax.dot_general(
        scaled, col_pts, (((0,), (0,)), ((), ())), preferred_element_type=jnp.float32
    )
    dist2 = jnp.maximum(sq_norms[0][:, None] + col_sq[0][None, :] - 2.0 * cross, 0.0)
    radius = jnp.sqrt(dist2)
    values = (1.0 + root_five * radius + 5.0 / 3.0 * dist2) * jnp.exp(-root_five * radius)
    return values.astype(jnp.bfloat16)


def forward_term(col_dirs, kernel):
    return lax.dot_general(
        col_dirs, kernel, (((1,), (1,)), ((), ())), preferred_element_type=jnp.float32
    )


def on_device(points, lengthscale, noise, solution, residual, direction):
    row_count = points.shape[1]
    scaled = (points / lengthscale[:, None]).astype(jnp.bfloat16)
    wide = scaled.astype(jnp.float32)
    sq_norms = jnp.sum(wide * wide, axis=0)[None, :]
    dir_bf = direction.astype(jnp.bfloat16)

    def one_block(block_pts, block_sq, block_dirs):
        kernel = kernel_tile(scaled, sq_norms, block_pts, block_sq)
        return (kernel, forward_term(block_dirs, kernel))

    totals = jnp.zeros((dir_bf.shape[0], row_count), jnp.float32)
    many_pts = lax.all_gather(scaled, "blk", axis=1, tiled=True)
    many_sq = lax.all_gather(sq_norms.astype(jnp.bfloat16), "blk", axis=1, tiled=True).astype(
        jnp.float32
    )
    many_dirs = lax.all_gather(dir_bf, "blk", axis=1, tiled=True)
    shards = many_pts.shape[1] // row_count

    def per_shard(carry, index):
        first = index * row_count
        block_pts = lax.dynamic_slice_in_dim(many_pts, first, row_count, 1)
        block_sq = lax.dynamic_slice_in_dim(many_sq, first, row_count, 1)
        block_dirs = lax.dynamic_slice_in_dim(many_dirs, first, row_count, 1)
        unused, term = one_block(block_pts, block_sq, block_dirs)
        return (carry + term, None)

    result, unused = lax.scan(per_shard, totals, jnp.arange(shards, dtype=jnp.int32))
    totals = result
    image = totals + noise[0] * direction
    rr_old, curv = lax.psum(
        (jnp.sum(residual * residual, axis=1), jnp.sum(direction * image, axis=1)), "blk"
    )
    alpha = rr_old / curv
    new_residual = residual - alpha[:, None] * image
    rr_new = lax.psum(jnp.sum(new_residual * new_residual, axis=1), "blk")
    new_solution = solution + alpha[:, None] * direction
    new_direction = new_residual + (rr_new / rr_old)[:, None] * direction
    return (new_solution, new_residual, new_direction)


def solution(mesh):
    in_specs = (P(None, "blk"), P(), P(), P("rep", "blk"), P("rep", "blk"), P("rep", "blk"))
    out_specs = (P("rep", "blk"), P("rep", "blk"), P("rep", "blk"))
    return jax.shard_map(
        on_device, mesh=mesh, in_specs=in_specs, out_specs=out_specs, check_vma=False
    )
```

profile of v0, /device:TPU:0, one launch (start us, length us, event | category | flops | bytes accessed | tf_op | source)
XLA Modules:
  0.0 500.1 jit_solution(14381817789451925909)
XLA Ops:
  7.2 1.6 multiply_reduce_fusion
  8.9 83.0 %all-gather = bf16[32768]{0:T(1024)(128)(2,1)S(1)} all-gather(bf16[1024]{0:T(1024)(128)(2,1)S(1)} %convert_element_type.32), channel_id=2, replica_groups=mesh['blk'=32,'rep'=4] {'blk'}, dimensions={0}, use_global_device_ids=true | all-gather | bytes 67584 | tf_op jit(solution)/shard_map/all_gather | solution.py:40
  91.9 0.7 convert_element_type.29
  93.3 77.1 %all_gather.9 = bf16[4,32768]{1,0:T(4,128)(2,1)S(1)} all-gather(bf16[4,1024]{1,0:T(4,128)(2,1)S(1)} %convert_element_type.29), channel_id=1, replica_groups=mesh['blk'=32,'rep'=4] {'blk'}, dimensions={1}, use_global_device_ids=true | all-gather | bytes 270336 | tf_op jit(solution)/shard_map/all_gather | solution.py:43
  170.4 165.5 %while.11 = (s32[]{:T(128)}, f32[4,1024]{1,0:T(4,128)S(1)}, s32[32]{0:T(128)S(1)}, bf16[4,32768]{1,0:T(4,128)(2,1)S(1)}, f32[1024]{0:T(1024)S(1)}, /*index=5*/f3...) while((s32[]{:T(128)}, f32[4,1024]{1,0:T(4,128)S(1)}, ...), condition=%wide.region_4.5_spmd.clone, body=%wide.region_3.4_spmd.clone.sunk | while | flops 87040008 | bytes 190140 | solution.py:54
  171.7 3.9 fusion.22
  175.6 0.6 dynamic_slice.30
  176.9 3.9 fusion.22
  180.8 0.6 dynamic_slice.30
  182.0 3.9 fusion.22
  185.9 0.6 dynamic_slice.30
  187.2 3.9 fusion.22
  191.1 0.6 dynamic_slice.30
  192.4 3.9 fusion.22
  196.3 0.6 dynamic_slice.30
  197.5 3.9 fusion.22
  201.4 0.6 dynamic_slice.30
  202.7 3.9 fusion.22
  207.9 3.9 fusion.22
  213.0 3.9 fusion.22
  218.2 3.9 fusion.22
  223.4 3.9 fusion.22
  228.6 3.9 fusion.22
  233.7 3.9 fusion.22
  238.9 3.9 fusion.22
  244.1 3.9 fusion.22
  249.2 3.9 fusion.22
  254.4 3.9 fusion.22
  259.6 3.9 fusion.22
  264.8 3.9 fusion.22
  269.9 3.9 fusion.22
  275.1 3.9 fusion.22
  280.3 3.9 fusion.22
  285.4 3.9 fusion.22
  290.6 3.9 fusion.22
  295.8 3.9 fusion.22
  299.7 0.6 dynamic_slice.30
  300.9 3.9 fusion.22
  306.1 3.9 fusion.22
  311.3 3.9 fusion.22
  316.5 3.9 fusion.22
  321.6 3.9 fusion.22
  326.8 3.9 fusion.22
  332.0 3.9 fusion.22
  336.0 78.9 %all-reduce = (f32[4]{0:T(128)S(1)}, f32[4]{0:T(128)S(1)}) all-reduce(f32[4]{0:T(128)S(1)} %get-tuple-element.97, f32[4]{0:T(128)S(1)} %get-tuple-element.96), channel_id=1, replica_groups=mesh['blk'=32,'rep'=4] {'blk'}, use_global_device_ids=true, to_apply=%region_1.2 | all-reduce | flops 8 | bytes 64 | tf_op jit(solution)/shard_map/psum | solution.py:57
  414.9 0.8 multiply_reduce_fusion.1
  415.7 76.8 %psum.23 = f32[4]{0:T(128)S(1)} all-reduce(f32[4]{0:T(128)S(1)} %get-tuple-element.91), channel_id=1, replica_groups=mesh['blk'=32,'rep'=4] {'blk'}, use_global_device_ids=true, to_apply=%region_8.9 | all-reduce | flops 4 | bytes 32 | tf_op jit(solution)/shard_map/psum | solution.py:62
  492.6 0.7 multiply_add_fusion
  (75 shorter events, 15.2 us)
Async XLA Ops:
  7.2 163.2 %all-gather.3.cloned.1.call-start = ((), (), s32[]{:S(2)}) async-start(), calls=%async_computation | async-start | bytes 2162688 | tf_op jit(solution)/shard_map/all_gather | solution.py:39
  170.4 165.5 %copy-start = (f32[4,1024]{1,0:T(4,128)S(1)}, f32[4,1024]{1,0:T(4,128)}, u32[]{:S(2)}) copy-start(f32[4,1024]{1,0:T(4,128)} %param.13) | copy-start | bytes 49156
  170.4 165.5 %copy-start.1 = (f32[4,1024]{1,0:T(4,128)S(1)}, f32[4,1024]{1,0:T(4,128)}, u32[]{:S(2)}) copy-start(f32[4,1024]{1,0:T(4,128)} %param.12) | copy-start | bytes 49156
  170.4 244.5 %copy-start.3 = (f32[4,1024]{1,0:T(4,128)S(1)}, f32[4,1024]{1,0:T(4,128)}, u32[]{:S(2)}) copy-start(f32[4,1024]{1,0:T(4,128)} %param.11) | copy-start | bytes 49156
  415.7 77.5 %copy-start.2 = (f32[4,1024]{1,0:T(4,128)}, f32[4,1024]{1,0:T(4,128)S(1)}, u32[]{:S(2)}) copy-start(f32[4,1024]{1,0:T(4,128)S(1)} %get-tuple-element.92) | copy-start | bytes 49156
Sparse Core Ops, SparseCore 0:
  9.6 155.8 all-gather.2
where the time goes:
time: 503 us; the launch traced here: 500 us
  blocking collectives  316 us (63%)
  matrix products  125 us (25%)
  loops' own time  21.5 us (4%)
  local copies, waits for them, and re-layouts  19.1 us (4%)
  between operations  14.7 us (3%)
    dot_general x32, matrix products, forward_term(): lax.dot_general(col_dirs, kernel, (((1,), (1,)), ((), ())), preferred_ele...  125 us
    all_gather x1, blocking collectives, on_device(): lax.all_gather(sq_norms.astype(jnp.bfloat16), 'blk', axis=1, tiled=True)  83 us
    psum x1, blocking collectives, on_device(): lax.psum((jnp.sum(residual * residual, axis=1), jnp.sum(direction * image...  78.9 us
    all_gather x1, blocking collectives, on_device(): many_dirs = lax.all_gather(dir_bf, 'blk', axis=1, tiled=True)  77.1 us
    psum x1, blocking collectives, on_device(): rr_new = lax.psum(jnp.sum(new_residual * new_residual, axis=1), 'blk')  76.8 us
    another operation x1, loops' own time, on_device(): lax.scan(per_shard, totals, jnp.arange(shards, dtype=jnp.int32))  21.5 us
    dynamic_slice x32, local copies, waits for them, and re-layouts, on_device(): lax.scan(per_shard, totals, jnp.arange(shards, dtype=jnp.int32))  18.8 us
  transfers between devices with their start and end apart: 1, of which 0 were waited for; matrix products, arithmetic and copies ran while one was open for 0% of the time, Pallas kernels for 0%

commit v1 on v0

v1 whole, which is shorter than its diff:
```python
import math

import jax
import jax.numpy as jnp
from jax import lax
from jax.experimental import pallas as pl
from jax.experimental.pallas import tpu as pltpu
from jax.sharding import PartitionSpec as P

MESH = pl.DeviceIdType.MESH
bf16 = jnp.bfloat16
f32 = jnp.float32
BLOCK = 1024
TILE = 512
OFFSETS = ((0, 1), (1, 0), (1, 1), (1, 3), (1, 2), (2, 1), (2, 2), (0, 2), (2, 0))
SCALE = math.sqrt(5.0) / 3.0


def matern(dist):
    dist = jnp.maximum(dist, 1e-30)
    root = dist * lax.rsqrt(dist)
    decay = jnp.exp2(root * (-3.0 / math.log(2.0)))
    return ((root + dist + 1.0 / 3.0) * decay).astype(bf16)


def pick(index, values):
    result = jnp.int32(values[0])
    for k in range(1, len(values)):
        result = jnp.where(index == k, jnp.int32(values[k]), result)
    return result


def squares(points):
    wide = points.astype(f32)
    total = jnp.sum(wide * wide, axis=0, keepdims=True)
    high = total.astype(bf16).astype(f32)
    rest = total - high
    mid = rest.astype(bf16).astype(f32)
    return (high, mid, rest - mid)


def kernel(
    points_ref, length_ref, noise_ref, sol_ref, res_ref, dir_ref,
    out_sol, out_res, out_dir,
    pts, dirs, dmat, amat, first, second, parts, got, sums1, sums2,
    pts_send, pts_recv, dir_send, dir_recv, part_send, part_recv, sum_send, sum_recv,
):
    blk = lax.axis_index("blk")
    rep = lax.axis_index("rep")
    ylo = blk % 2
    col = blk // 2
    x = col // 4
    z = col % 4
    me = ylo * 4 + rep
    dx1 = pick(me, [d[0] for d in OFFSETS[:8]])
    dz1 = pick(me, [d[1] for d in OFFSETS[:8]])
    dx2, dz2 = OFFSETS[8]

    def column(dx, dz):
        return ((x + dx + 4) % 4) * 4 + (z + dz + 4) % 4

    def member(c, k):
        return (c * 2 + k // 4, k % 4)

    other1 = column(dx1, dz1)
    other2 = column(dx2, dz2)
    mates = [member(col, (me + m) % 8) for m in range(1, 8)]
    users = [member(column(-d[0], -d[1]), min(k, 7)) for k, d in enumerate(OFFSETS)]
    peers1 = []
    for m in range(1, 8):
        e = (x * 2 + ylo + m) % 8
        peers1.append((((e // 2) * 4 + z) * 2 + e % 2, rep))
    peers2 = [((x * 4 + (z + m) % 4) * 2 + ylo, rep) for m in range(1, 4)]

    barrier = pltpu.get_barrier_semaphore()
    sources1 = [member(other1, k) for k in range(8)]
    sources2 = [member(other2, k) for k in range(8)]

    def hail(device):
        pl.semaphore_signal(barrier, inc=1, device_id=device, device_id_type=MESH)

    for device in mates + users + sources1 + peers1 + peers2:
        hail(device)

    @pl.when(me == 7)
    def _():
        for device in sources2:
            hail(device)

    row = lax.broadcasted_iota(jnp.int32, (32, 32), 0)
    lane = lax.broadcasted_iota(jnp.int32, (32, 32), 1)
    length = jnp.sum(jnp.where(row == lane, length_ref[...], 0.0), axis=1, keepdims=True)
    pts[ylo, 0:32, :] = (points_ref[...] * (SCALE / length)).astype(bf16)
    direction = dir_ref[...]
    dirs[me] = jnp.concatenate(
        [direction[:, c * 256 : (c + 1) * 256] for c in range(4)], axis=0
    ).astype(bf16)

    pl.semaphore_wait(barrier, 34 + 8 * jnp.where(me == 7, 1, 0))

    def send(src, dst, send_sem, recv_sem, device):
        copy = pltpu.make_async_remote_copy(
            src_ref=src, dst_ref=dst, send_sem=send_sem, recv_sem=recv_sem,
            device_id=device, device_id_type=MESH,
        )
        copy.start()
        return copy

    def send_points(slot, device, k):
        place = slot * 2 + ylo
        return send(
            pts.at[ylo, pl.ds(0, 32)], pts.at[place, pl.ds(0, 32)], pts_send.at[k], pts_recv.at[place], device
        )

    def user_of(k):
        return member(column(-pick(k, [d[0] for d in OFFSETS[:8]]), -pick(k, [d[1] for d in OFFSETS[:8]])), k)

    waits = []
    waits.append(send_points(0, (blk + 1 - 2 * ylo, rep), 0))
    waits.append(send_points(1, user_of(rep), 1))
    waits.append(send_points(1, user_of(rep + 4), 2))

    @pl.when(rep == 0)
    def _():
        send_points(2, users[8], 3)

    for m in range(7):
        waits.append(send(dirs.at[me], dirs.at[me], dir_send.at[m], dir_recv.at[me], mates[m]))
    for k in range(9):
        place = (1 if k < 8 else 2) * 8 + me
        waits.append(send(dirs.at[me], dirs.at[place], dir_send.at[7 + k], dir_recv.at[place], users[k]))

    first[...] = jnp.zeros_like(first)
    second[...] = jnp.zeros_like(second)

    def take_points(place):
        pltpu.make_async_copy(pts.at[place, pl.ds(0, 32)], pts.at[place, pl.ds(0, 32)], pts_recv.at[place]).wait()

    def take_dirs(place):
        pltpu.make_async_copy(dirs.at[place], dirs.at[place], dir_recv.at[place]).wait()

    def augment(place):
        high, mid, low = squares(pts[place, 0:32, :])
        one = jnp.ones((1, BLOCK), f32)
        extra = jnp.concatenate([high, mid, low, one, one, one, jnp.zeros((10, BLOCK), f32)], axis=0)
        pts[place, 32:48, :] = extra.astype(bf16)

    def own_rows(place):
        q = pts[place, 0:32, :]
        high, mid, low = squares(q)
        one = jnp.ones((1, BLOCK), f32)
        whole = jnp.concatenate(
            [q.astype(f32) * -2.0, one, one, one, high, mid, low, jnp.zeros((10, BLOCK), f32)], axis=0
        )
        amat[place] = jnp.transpose(whole).astype(bf16)

    def spread(place):
        pieces = [dirs[place * 4 + r].astype(f32) for r in range(4)]
        for c in range(4):
            rows = jnp.concatenate([p[c * 4 : c * 4 + 4, :] for p in pieces], axis=0)
            dmat[place, :, c * 256 : (c + 1) * 256] = rows.astype(bf16)

    take_points(1 - ylo)
    for place in range(2):
        augment(place)
        own_rows(place)
    for m in range(1, 8):
        take_dirs((me + m) % 8)
    for place in range(2):
        spread(place)

    def arrive(slot):
        for y in range(2):
            take_points(slot * 2 + y)
            augment(slot * 2 + y)
        for k in range(8):
            take_dirs(slot * 8 + k)
        for y in range(2):
            spread(slot * 2 + y)

    arrive(1)

    @pl.when(me == 7)
    def _():
        arrive(2)

    early1 = jnp.where(col < other1, 0, 2)
    early2 = jnp.where(col < other2, 0, 2)

    def half(u, early):
        i = jnp.where(u < 4, 0, early) + (u // 2) % 2
        j = jnp.where(u < 4, 2, early) + u % 2
        return i, j

    def tile(t):
        hi, hj = half(t % 8, jnp.where(t < 8, early1, early2))
        v = t - 8
        w = v - 4
        di = jnp.where(v < 4, v, jnp.where(w < 3, 0, jnp.where(w < 5, 1, 2)))
        dj = jnp.where(v < 4, v, jnp.where(w < 3, w + 1, jnp.where(w < 5, w - 1, 3)))
        diag = jnp.logical_and(me == 6, t >= 8)
        i = jnp.where(me < 6, t // 4, jnp.where(diag, di, hi))
        j = jnp.where(me < 6, 4 + t % 4, jnp.where(diag, dj, jnp.where(t < 8, 4, 8) + hj))
        same = jnp.logical_and(diag, v < 4)
        return i, j, same

    def step(t, carry):
        i, j, same = tile(t)
        ib, i0 = i // 2, pl.multiple_of((i % 2) * TILE, TILE)
        jb, j0 = j // 2, pl.multiple_of((j % 2) * TILE, TILE)
        dist = jnp.dot(
            amat[ib, pl.ds(i0, TILE), :], pts[jb, :, pl.ds(j0, TILE)], preferred_element_type=f32
        )
        values = matern(dist)
        weight = jnp.where(same, 0.5, 1.0).astype(bf16)
        di = dmat[ib, :, pl.ds(i0, TILE)] * weight
        dj = dmat[jb, :, pl.ds(j0, TILE)] * weight
        first[ib, :, pl.ds(i0, TILE)] += lax.dot_general(
            dj, values, (((1,), (1,)), ((), ())), preferred_element_type=f32
        )
        second[jb, :, pl.ds(j0, TILE)] += jnp.dot(di, values, preferred_element_type=f32)
        return carry

    lax.fori_loop(0, 16 + 2 * jnp.where(me == 6, 1, 0), step, 0)

    def pack(place, whole):
        for r in range(4):
            piece = [whole[r * 4 : r * 4 + 4, c * 256 : (c + 1) * 256] for c in range(4)]
            parts[place * 4 + r] = jnp.concatenate(piece, axis=0).astype(bf16)

    for y in range(2):
        pack(2 + y, second[2 + y])
    for k in range(8):
        waits.append(send(parts.at[8 + k], got.at[8 + me], part_send.at[8 + k], part_recv.at[8 + me], sources1[k]))

    @pl.when(me == 7)
    def _():
        for y in range(2):
            pack(4 + y, second[4 + y])
        for k in range(8):
            send(parts.at[16 + k], got.at[16], part_send.at[16 + k], part_recv.at[16], sources2[k])

    for y in range(2):
        pack(y, first[y] + second[y])
    for m in range(7):
        k = (me + m + 1) % 8
        waits.append(send(parts.at[k], got.at[me], part_send.at[k], part_recv.at[me], mates[m]))

    total = parts[me].astype(f32)
    for k in range(17):
        def take_part():
            pltpu.make_async_copy(got.at[k], got.at[k], part_recv.at[k]).wait()
        if k < 8:
            got_k = (me + k) % 8
            if k == 0:
                continue
            pltpu.make_async_copy(got.at[got_k], got.at[got_k], part_recv.at[got_k]).wait()
            total += got[got_k].astype(f32)
        else:
            take_part()
            total += got[k].astype(f32)

    product = jnp.concatenate([total[c * 4 : c * 4 + 4, :] for c in range(4)], axis=1)
    image = 3.0 * product + noise_ref[0] * direction
    residual = res_ref[...]

    def lanes(a):
        result = a[:, 0:128]
        for c in range(1, 8):
            result += a[:, c * 128 : (c + 1) * 128]
        return result

    e = x * 2 + ylo
    sums1[e] = jnp.concatenate(
        [lanes(residual * residual), lanes(direction * image), lanes(residual * image), lanes(image * image)], axis=0
    )
    for m in range(7):
        waits.append(send(sums1.at[e], sums1.at[e], sum_send.at[m], sum_recv.at[e], peers1[m]))
    for m in range(1, 8):
        place = (e + m) % 8
        pltpu.make_async_copy(sums1.at[place], sums1.at[place], sum_recv.at[place]).wait()
    sums2[z] = sum(sums1[k] for k in range(8))
    for m in range(3):
        waits.append(send(sums2.at[z], sums2.at[z], sum_send.at[7 + m], sum_recv.at[8 + z], peers2[m]))
    for m in range(1, 4):
        place = (z + m) % 4
        pltpu.make_async_copy(sums2.at[place], sums2.at[place], sum_recv.at[8 + place]).wait()
    stats = jnp.sum(sum(sums2[k] for k in range(4)), axis=1, keepdims=True)
    rr, curv, cross, norm = stats[0:4], stats[4:8], stats[8:12], stats[12:16]
    alpha = rr / curv
    rr_new = jnp.maximum(rr - 2.0 * alpha * cross + alpha * alpha * norm, 0.0)
    new_res = residual - alpha * image
    out_sol[...] = sol_ref[...] + alpha * direction
    out_res[...] = new_res
    out_dir[...] = new_res + (rr_new / rr) * direction

    for copy in waits:
        copy.wait_send()

    @pl.when(rep == 0)
    def _():
        pltpu.make_async_copy(pts.at[0, pl.ds(0, 32)], pts.at[0, pl.ds(0, 32)], pts_send.at[3]).wait()

    @pl.when(me == 7)
    def _():
        for k in range(8):
            pltpu.make_async_copy(parts.at[k], parts.at[k], part_send.at[16 + k]).wait()


def on_device(points, lengthscale, noise, solution, residual, direction):
    vmem = pl.BlockSpec(memory_space=pltpu.VMEM)
    dma = pltpu.SemaphoreType.DMA
    return pl.pallas_call(
        kernel,
        out_shape=[jax.ShapeDtypeStruct(direction.shape, f32)] * 3,
        in_specs=[vmem, vmem, pl.BlockSpec(memory_space=pltpu.SMEM), vmem, vmem, vmem],
        out_specs=[vmem] * 3,
        scratch_shapes=[
            pltpu.VMEM((6, 48, BLOCK), bf16),
            pltpu.VMEM((24, 16, 256), bf16),
            pltpu.VMEM((6, 16, BLOCK), bf16),
            pltpu.VMEM((2, BLOCK, 48), bf16),
            pltpu.VMEM((2, 16, BLOCK), f32),
            pltpu.VMEM((6, 16, BLOCK), f32),
            pltpu.VMEM((24, 16, 256), bf16),
            pltpu.VMEM((17, 16, 256), bf16),
            pltpu.VMEM((8, 16, 128), f32),
            pltpu.VMEM((4, 16, 128), f32),
            dma((4,)), dma((6,)), dma((16,)), dma((24,)), dma((24,)), dma((17,)), dma((10,)), dma((12,)),
        ],
        compiler_params=pltpu.CompilerParams(
            collective_id=0, has_side_effects=True, vmem_limit_bytes=40 * 2**20
        ),
        cost_estimate=pl.CostEstimate(flops=2**31, bytes_accessed=2**20, transcendentals=2**23),
    )(points, lengthscale.reshape(1, 32), noise, solution, residual, direction)


def solution(mesh):
    in_specs = (P(None, "blk"), P(), P(), P("rep", "blk"), P("rep", "blk"), P("rep", "blk"))
    out_specs = (P("rep", "blk"), P("rep", "blk"), P("rep", "blk"))
    return jax.shard_map(
        on_device, mesh=mesh, in_specs=in_specs, out_specs=out_specs, check_vma=False
    )
```

time: 503 us -> 50.1 us (0.10)
  blocking collectives: 316 us -> 0 us
  matrix products: 125 us -> 0 us
  Pallas kernels: 0 us -> 42.9 us
  loops' own time: 21.5 us -> 0 us
  local copies, waits for them, and re-layouts: 19.1 us -> 5.52 us
  between operations: 14.7 us -> 1.3 us
    all_gather x2 -> x0, blocking collectives: 160 us -> none  [the longest x1 83 us: on_device(): lax.all_gather(sq_norms.astype(jnp.bfloat16), 'blk', axis=1, tiled=True)]
    psum x2 -> x0, blocking collectives: 156 us -> none  [the longest x1 78.9 us: on_device(): lax.psum((jnp.sum(residual * residual, axis=1), jnp.sum(direction * image...]
    dot_general x32 -> x0, matrix products: 125 us -> none  [forward_term(): lax.dot_general(col_dirs, kernel, (((1,), (1,)), ((), ())), preferred_ele...]
    pallas_call x0 -> x1, Pallas kernels: none -> 42.9 us  [on_device(): pl.pallas_call(kernel, out_shape=[jax.ShapeDtypeStruct(direction.shape, f...]
    another operation x1 -> x0, loops' own time: 21.5 us -> none  [on_device(): lax.scan(per_shard, totals, jnp.arange(shards, dtype=jnp.int32))]
    dynamic_slice x64 -> x0, local copies, waits for them, and re-layouts: 19.1 us -> none  [the longest x32 18.8 us: on_device(): lax.scan(per_shard, totals, jnp.arange(shards, dtype=jnp.int32))]
    unnamed x8 -> x13, local copies, waits for them, and re-layouts: 0.02 us -> 5.52 us
  transfers between devices with their start and end apart: 1 -> 0, of which waited for: 0 -> 0; matrix products, arithmetic and copies ran while one was open for 0% -> 0% of each run, Pallas kernels for 0% -> 0%
where the time goes in v1:
time: 50.1 us; the launch traced here: 49.8 us
  Pallas kernels  42.9 us (86%)
  local copies, waits for them, and re-layouts  5.52 us (11%)
  between operations  1.3 us (3%)
    pallas_call x1, Pallas kernels, on_device(): pl.pallas_call(kernel, out_shape=[jax.ShapeDtypeStruct(direction.shape, f...  42.9 us
    unnamed x13, local copies, waits for them, and re-layouts  5.52 us

profile of v1, /device:TPU:0, one launch (start us, length us, event | category | flops | bytes accessed | tf_op | source)
XLA Modules:
  0.0 49.8 jit_solution(6918814910949764500)
XLA Ops:
  1.3 0.0 copy-start.4
  1.3 0.6 %copy-done.4 = f32[32]{0:T(128)S(1)} copy-done((f32[32]{0:T(128)S(1)}, f32[32]{0:T(128)}, u32[]{:S(2)}) %copy-start.4) | copy-done | bytes 152
  1.9 0.0 copy-start
  1.9 0.9 %copy-done = f32[32,1024]{1,0:T(8,128)S(1)} copy-done((f32[32,1024]{1,0:T(8,128)S(1)}, f32[32,1024]{1,0:T(8,128)}, u32[]{:S(2)}) %copy-start) | copy-done | bytes 131096
  2.8 0.0 copy-start.1
  2.8 0.7 %copy-done.1 = f32[4,1024]{1,0:T(4,128)S(1)} copy-done((f32[4,1024]{1,0:T(4,128)S(1)}, f32[4,1024]{1,0:T(4,128)}, u32[]{:S(2)}) %copy-start.1) | copy-done | bytes 16408
  3.6 0.0 copy-start.2
  3.6 0.7 %copy-done.2 = f32[4,1024]{1,0:T(4,128)S(1)} copy-done((f32[4,1024]{1,0:T(4,128)S(1)}, f32[4,1024]{1,0:T(4,128)}, u32[]{:S(2)}) %copy-start.2) | copy-done | bytes 16408
  4.3 0.0 copy-start.3
  4.3 0.7 %copy-done.3 = f32[4,1024]{1,0:T(4,128)S(1)} copy-done((f32[4,1024]{1,0:T(4,128)S(1)}, f32[4,1024]{1,0:T(4,128)}, u32[]{:S(2)}) %copy-start.3) | copy-done | bytes 16408
  5.0 42.9 %shard_map.85 = (f32[4,1024]{1,0:T(4,128)S(1)}, f32[4,1024]{1,0:T(4,128)S(1)}, f32[4,1024]{1,0:T(4,128)S(1)}) custom-call(f32[32,1024]{1,0:T(8,128)S(1)} %copy-done, f32[1,32]{1,0:T(1,128)S(1)} %bitcast.1, f32[1]{0:T(128)S(6)} %copy.12.noise_ref, f32[4,1024]{1,0:T(4,128)S(1)} %copy-done.1, f32[4,1024]{1,0:T(4,128)S(1)} %copy-done.2, f32[4,1024]{1,0:T(4,128)S(1)} %copy-done.3), custom_call_target="tpu_custom_call" | custom-call | flops 2147483648 | bytes 1048576 | tf_op jit(solution)/shard_map/pallas_call | solution.py:313
  47.9 0.6 %copy.13 = f32[4,1024]{1,0:T(4,128)} copy(f32[4,1024]{1,0:T(4,128)S(1)} %get-tuple-element.6) | data formatting | bytes 32768
  48.5 0.6 %copy.14 = f32[4,1024]{1,0:T(4,128)} copy(f32[4,1024]{1,0:T(4,128)S(1)} %get-tuple-element.7) | data formatting | bytes 32768
  49.2 0.6 %copy.15 = f32[4,1024]{1,0:T(4,128)} copy(f32[4,1024]{1,0:T(4,128)S(1)} %get-tuple-element.8) | data formatting | bytes 32768
Async XLA Ops:
  1.3 0.7 %copy-start.4 = (f32[32]{0:T(128)S(1)}, f32[32]{0:T(128)}, u32[]{:S(2)}) copy-start(f32[32]{0:T(128)} %param.7) | copy-start | bytes 388
  1.9 0.9 %copy-start = (f32[32,1024]{1,0:T(8,128)S(1)}, f32[32,1024]{1,0:T(8,128)}, u32[]{:S(2)}) copy-start(f32[32,1024]{1,0:T(8,128)} %points_ref.1) | copy-start | bytes 393220
  2.8 0.7 %copy-start.1 = (f32[4,1024]{1,0:T(4,128)S(1)}, f32[4,1024]{1,0:T(4,128)}, u32[]{:S(2)}) copy-start(f32[4,1024]{1,0:T(4,128)} %sol_ref.1) | copy-start | bytes 49156
  3.6 0.7 %copy-start.2 = (f32[4,1024]{1,0:T(4,128)S(1)}, f32[4,1024]{1,0:T(4,128)}, u32[]{:S(2)}) copy-start(f32[4,1024]{1,0:T(4,128)} %res_ref.1) | copy-start | bytes 49156
  4.3 0.7 %copy-start.3 = (f32[4,1024]{1,0:T(4,128)S(1)}, f32[4,1024]{1,0:T(4,128)}, u32[]{:S(2)}) copy-start(f32[4,1024]{1,0:T(4,128)} %dir_ref.1) | copy-start | bytes 49156

commit v2 on v0

v2 whole, which is shorter than its diff:
```python
import math

import jax
import jax.numpy as jnp
from jax import lax
from jax.experimental import pallas as pl
from jax.experimental.pallas import tpu as pltpu
from jax.sharding import PartitionSpec as P

MESH = pl.DeviceIdType.MESH
bf16 = jnp.bfloat16
f32 = jnp.float32
BLOCK = 1024
ROWS = 512
COLS = 256
SCALE = math.sqrt(5.0) / 3.0
SLOTS = (
    ((0, 0), (0, 1), None, None),
    ((0, 0), (1, 0), None, None),
    ((-1, 0), (0, 1), None, None),
    ((-1, 0), (0, -1), None, None),
    ((0, -1), (1, 1), None, None),
    ((-1, 0), (1, 1), None, None),
    ((0, 0), None, (-1, -1), (1, 1)),
    ((0, -1), (0, 1), (-1, 0), (1, 0)),
)
USES = tuple((m, s) + SLOTS[m][s] for m in range(8) for s in range(4) if SLOTS[m][s] is not None)


def use_of(m, s):
    for index, use in enumerate(USES):
        if use[:2] == (m, s):
            return index
    return 0


def matern(dist):
    dist = jnp.maximum(dist, 1e-30)
    root = dist * lax.rsqrt(dist)
    decay = jnp.exp2(root * (-3.0 / math.log(2.0)))
    return ((root + dist + 1.0 / 3.0) * decay).astype(bf16)


def pick(index, values):
    result = jnp.int32(values[0])
    for k in range(1, len(values)):
        if values[k] != values[0]:
            result = jnp.where(index == k, jnp.int32(values[k]), result)
    return result


def squares(points):
    wide = points.astype(f32)
    total = jnp.sum(wide * wide, axis=0, keepdims=True)
    high = total.astype(bf16).astype(f32)
    rest = total - high
    mid = rest.astype(bf16).astype(f32)
    return (high, mid, rest - mid)


def kernel(
    points_hbm, length_hbm, noise_hbm, sol_hbm, res_hbm, dir_hbm,
    out_sol, out_res, out_dir,
    points_ref, length_ref, noise_ref, sol_ref, res_ref, dir_ref,
    mine, mydir, pts, dirs, dmat, amat, even, odd, first, second, parts, got, sums,
    load, pts_send, pts_recv, dir_send, dir_recv, part_send, part_recv, sum_send, sum_recv,
):
    loads = [
        pltpu.make_async_copy(a, b, load.at[n])
        for n, (a, b) in enumerate(
            [
                (points_hbm, points_ref), (length_hbm, length_ref), (dir_hbm, dir_ref),
                (noise_hbm, noise_ref), (sol_hbm, sol_ref), (res_hbm, res_ref),
            ]
        )
    ]
    for copy in loads:
        copy.start()

    blk = lax.axis_index("blk")
    rep = lax.axis_index("rep")
    ylo = blk % 2
    col = blk // 2
    x = col // 4
    z = col % 4
    me = ylo * 4 + rep

    def column(dx, dz):
        return ((x + dx + 4) % 4) * 4 + (z + dz + 4) % 4

    def member(c, k):
        return (c * 2 + k // 4, k % 4)

    def slot_column(s):
        offsets = [SLOTS[m][s] or (0, 0) for m in range(8)]
        return column(pick(me, [d[0] for d in offsets]), pick(me, [d[1] for d in offsets]))

    slot_cols = [slot_column(s) for s in range(4)]
    slot_use = [pick(me, [use_of(m, s) for m in range(8)]) for s in range(4)]
    own_pair = jnp.logical_or(jnp.logical_or(me == 0, me == 1), me == 6)
    users = [member(column(-dx, -dz), m) for m, s, dx, dz in USES]
    peers = [((blk + m) % 32, rep) for m in range(1, 32)]

    barrier = pltpu.get_barrier_semaphore()

    def hail(device):
        pl.semaphore_signal(barrier, inc=1, device_id=device, device_id_type=MESH)

    def if_slot(s, action):
        if s == 0:
            action()
        elif s == 1:
            pl.when(me != 6)(action)
        else:
            pl.when(me >= 6)(action)

    def hail_sources(s):
        def action():
            for k in range(8):
                if s == 0:
                    @pl.when(jnp.logical_not(jnp.logical_and(own_pair, me == k)))
                    def _():
                        hail(member(slot_cols[s], k))
                else:
                    hail(member(slot_cols[s], k))
        return action

    for s in range(4):
        if_slot(s, hail_sources(s))
    for use, device in zip(USES, users):
        if use[2:] == (0, 0):
            @pl.when(me != use[0])
            def _():
                hail(device)
        else:
            hail(device)
    for device in peers:
        hail(device)

    for copy in loads[:3]:
        copy.wait()
    row = lax.broadcasted_iota(jnp.int32, (32, 32), 0)
    lane = lax.broadcasted_iota(jnp.int32, (32, 32), 1)
    length = jnp.sum(jnp.where(row == lane, length_ref[...], 0.0), axis=1, keepdims=True)
    mine[...] = (points_ref[...] * (SCALE / length)).astype(bf16)
    direction = dir_ref[...]
    mydir[...] = jnp.concatenate(
        [direction[:, c * 256 : (c + 1) * 256] for c in range(4)], axis=0
    ).astype(bf16)

    slots_used = jnp.where(me < 6, 2, jnp.where(me == 6, 3, 4))
    pl.semaphore_wait(barrier, 8 * slots_used + len(USES) + 31 - 2 * jnp.where(own_pair, 1, 0))

    def remote(src, dst, send_sem, recv_sem, device):
        return pltpu.make_async_remote_copy(
            src_ref=src, dst_ref=dst, send_sem=send_sem, recv_sem=recv_sem,
            device_id=device, device_id_type=MESH,
        )

    def deliver(src, dst, send_sem, recv_sem, device, is_self, start):
        def away():
            copy = remote(src, dst, send_sem, recv_sem, device)
            copy.start() if start else copy.wait_send()

        def here():
            if start:
                pltpu.make_async_copy(src, dst, recv_sem).start()

        if is_self is None:
            away()
        else:
            pl.when(is_self)(here)
            pl.when(jnp.logical_not(is_self))(away)

    def points_out(start):
        for r in range(4):
            @pl.when(rep == r)
            def _():
                index = 0
                for u, (m, s, dx, dz) in enumerate(USES):
                    if m % 4 == r:
                        place = s * 2 + ylo
                        deliver(
                            mine, pts.at[place, pl.ds(0, 32)], pts_send.at[index], pts_recv.at[place], users[u],
                            me == m if (dx, dz) == (0, 0) else None, start,
                        )
                        index += 1

    def dirs_out(start):
        for u, (m, s, dx, dz) in enumerate(USES):
            place = s * 8 + me
            deliver(
                mydir, dirs.at[place], dir_send.at[u], dir_recv.at[place], users[u],
                me == m if (dx, dz) == (0, 0) else None, start,
            )

    points_out(True)
    dirs_out(True)
    first[...] = jnp.zeros_like(first)
    second[...] = jnp.zeros_like(second)

    def augment(place):
        pltpu.make_async_copy(pts.at[place, pl.ds(0, 32)], pts.at[place, pl.ds(0, 32)], pts_recv.at[place]).wait()
        high, mid, low = squares(pts[place, 0:32, :])
        one = jnp.ones((1, BLOCK), f32)
        extra = jnp.concatenate([high, mid, low, one, one, one, jnp.zeros((10, BLOCK), f32)], axis=0)
        pts[place, 32:48, :] = extra.astype(bf16)

    def left_rows(place, y):
        q = pts[place, 0:32, :]
        high, mid, low = squares(q)
        one = jnp.ones((1, BLOCK), f32)
        whole = jnp.concatenate(
            [q.astype(f32) * -2.0, one, one, one, high, mid, low, jnp.zeros((10, BLOCK), f32)], axis=0
        )
        amat[y] = jnp.transpose(whole).astype(bf16)

    def spread(place):
        pieces = []
        for r in range(4):
            k = place * 4 + r
            pltpu.make_async_copy(dirs.at[k], dirs.at[k], dir_recv.at[k]).wait()
            pieces.append(dirs[k].astype(f32))
        for c in range(4):
            rows = jnp.concatenate([p[c * 4 : c * 4 + 4, :] for p in pieces], axis=0)
            dmat[place, :, c * 256 : (c + 1) * 256] = rows.astype(bf16)

    def pack(place, whole):
        for r in range(4):
            piece = [whole[r * 4 : r * 4 + 4, c * 256 : (c + 1) * 256] for c in range(4)]
            parts[place * 4 + r] = jnp.concatenate(piece, axis=0).astype(bf16)

    def parts_out(s, start):
        def action():
            for k in range(8):
                deliver(
                    parts.at[s * 8 + k], got.at[slot_use[s]], part_send.at[s * 8 + k], part_recv.at[slot_use[s]],
                    member(slot_cols[s], k), jnp.logical_and(own_pair, me == k) if s == 0 else None, start,
                )
        return action

    def phase(ph, carry):
        diag = jnp.logical_and(me == 6, ph == 0)
        left = ph * 4
        right = jnp.where(diag, 0, ph * 4 + 2)
        for y in range(2):
            augment(left + y)
            left_rows(left + y, y)

        @pl.when(jnp.logical_not(diag))
        def _():
            for y in range(2):
                augment(right + y)

        for y in range(2):
            spread(left + y)

        @pl.when(jnp.logical_not(diag))
        def _():
            for y in range(2):
                spread(right + y)

        low_col = jnp.where(ph == 0, slot_cols[0], slot_cols[2])
        high_col = jnp.where(ph == 0, slot_cols[1], slot_cols[3])
        early = jnp.where(low_col < high_col, 0, 1)
        count = jnp.where(me < 6, 32, jnp.where(diag, 20, 16))

        def tile(t):
            u = t - 8
            half_i = jnp.where(t < 8, t // 4, 2 * early + u // 4)
            half_j = jnp.where(t < 8, 4 + t % 4, 4 * early + t % 4)
            v = t // 2
            w = v - 4
            diag_i = jnp.where(v < 4, v, jnp.where(w < 3, 0, jnp.where(w < 5, 1, 2)))
            diag_j = jnp.where(v < 4, v, jnp.where(w < 3, w + 1, jnp.where(w < 5, w - 1, 3)))
            i = jnp.where(me < 6, t // 8, jnp.where(diag, diag_i, half_i))
            j = jnp.where(me < 6, t % 8, jnp.where(diag, diag_j * 2 + t % 2, half_j))
            return i, j, jnp.logical_and(diag, v < 4)

        def place(t):
            i, j, same = tile(t)
            i0 = pl.multiple_of((i % 2) * ROWS, ROWS)
            j0 = pl.multiple_of((j % 4) * COLS, COLS)
            return i // 2, i0, j // 4, j0, same

        def distances(t, out):
            ib, i0, jb, j0, same = place(jnp.minimum(t, count - 1))
            out[...] = jnp.dot(
                amat[ib, pl.ds(i0, ROWS), :], pts[right + jb, :, pl.ds(j0, COLS)], preferred_element_type=f32
            )

        def products(t, dist):
            ib, i0, jb, j0, same = place(t)
            values = matern(dist[...])
            weight = jnp.where(same, 0.5, 1.0).astype(bf16)
            di = dmat[left + ib, :, pl.ds(i0, ROWS)] * weight
            dj = dmat[right + jb, :, pl.ds(j0, COLS)] * weight
            first[ph * 2 + ib, :, pl.ds(i0, ROWS)] += lax.dot_general(
                dj, values, (((1,), (1,)), ((), ())), preferred_element_type=f32
            )
            second[ph * 2 + jb, :, pl.ds(j0, COLS)] += jnp.dot(di, values, preferred_element_type=f32)

        distances(0, even)

        def step(n, carry):
            for m in range(2):
                t = n * 4 + m * 2
                distances(t + 1, odd)
                products(t, even)
                distances(t + 2, even)
                products(t + 1, odd)
            return carry

        lax.fori_loop(0, count // 4, step, 0)

        @pl.when(diag)
        def _():
            for y in range(2):
                pack(y, first[y] + second[y])

        @pl.when(jnp.logical_not(diag))
        def _():
            for y in range(2):
                pack(left + y, first[ph * 2 + y])
                pack(right + y, second[ph * 2 + y])

        @pl.when(ph == 0)
        def _():
            for s in (0, 1):
                if_slot(s, parts_out(s, True))

        @pl.when(ph == 1)
        def _():
            for s in (2, 3):
                parts_out(s, True)()

        return carry

    lax.fori_loop(0, jnp.where(me < 6, 1, 2), phase, 0)

    for copy in loads[3:]:
        copy.wait()
    residual = res_ref[...]

    total = jnp.zeros((16, 256), f32)
    for u in range(len(USES)):
        pltpu.make_async_copy(got.at[u], got.at[u], part_recv.at[u]).wait()
        total += got[u].astype(f32)
    product = jnp.concatenate([total[c * 4 : c * 4 + 4, :] for c in range(4)], axis=1)
    image = 3.0 * product + noise_ref[0] * direction

    stats = jnp.concatenate(
        [
            jnp.sum(a, axis=1, keepdims=True)
            for a in (residual * residual, direction * image, residual * image, image * image)
        ],
        axis=0,
    )
    row = lax.broadcasted_iota(jnp.int32, (16, 128), 0)
    lane = lax.broadcasted_iota(jnp.int32, (16, 128), 1)
    sums[blk] = jnp.sum(jnp.where(row == lane, stats, 0.0), axis=0, keepdims=True)
    copies = [
        remote(sums.at[blk], sums.at[blk], sum_send.at[m], sum_recv.at[blk], peers[m]) for m in range(31)
    ]
    for copy in copies:
        copy.start()
    for m in range(1, 32):
        k = (blk + m) % 32
        pltpu.make_async_copy(sums.at[k], sums.at[k], sum_recv.at[k]).wait()
    stats = jnp.sum(jnp.where(row == lane, jnp.sum(sums[...], axis=0), 0.0), axis=1, keepdims=True)
    rr, curv, cross, norm = stats[0:4], stats[4:8], stats[8:12], stats[12:16]
    alpha = rr / curv
    rr_new = jnp.maximum(rr - 2.0 * alpha * cross + alpha * alpha * norm, 0.0)
    new_res = residual - alpha * image
    out_sol[...] = sol_ref[...] + alpha * direction
    out_res[...] = new_res
    out_dir[...] = new_res + (rr_new / rr) * direction

    points_out(False)
    dirs_out(False)
    for s in range(4):
        if_slot(s, parts_out(s, False))
    for copy in copies:
        copy.wait_send()


def on_device(points, lengthscale, noise, solution, residual, direction):
    vmem = pl.BlockSpec(memory_space=pltpu.VMEM)
    hbm = pl.BlockSpec(memory_space=pltpu.HBM)
    dma = pltpu.SemaphoreType.DMA
    probes = direction.shape[0]
    return pl.pallas_call(
        kernel,
        out_shape=[jax.ShapeDtypeStruct(direction.shape, f32)] * 3,
        in_specs=[hbm] * 6,
        out_specs=[vmem] * 3,
        scratch_shapes=[
            pltpu.VMEM((32, BLOCK), f32),
            pltpu.VMEM((1, 32), f32),
            pltpu.SMEM((1,), f32),
            pltpu.VMEM((probes, BLOCK), f32),
            pltpu.VMEM((probes, BLOCK), f32),
            pltpu.VMEM((probes, BLOCK), f32),
            pltpu.VMEM((32, BLOCK), bf16),
            pltpu.VMEM((16, 256), bf16),
            pltpu.VMEM((8, 48, BLOCK), bf16),
            pltpu.VMEM((32, 16, 256), bf16),
            pltpu.VMEM((8, 16, BLOCK), bf16),
            pltpu.VMEM((2, BLOCK, 48), bf16),
            pltpu.VMEM((ROWS, COLS), f32),
            pltpu.VMEM((ROWS, COLS), f32),
            pltpu.VMEM((4, 16, BLOCK), f32),
            pltpu.VMEM((4, 16, BLOCK), f32),
            pltpu.VMEM((32, 16, 256), bf16),
            pltpu.VMEM((len(USES), 16, 256), bf16),
            pltpu.VMEM((32, 1, 128), f32),
            dma((6,)), dma((6,)), dma((8,)), dma((len(USES),)), dma((32,)), dma((32,)), dma((len(USES),)),
            dma((31,)), dma((32,)),
        ],
        compiler_params=pltpu.CompilerParams(
            collective_id=0, has_side_effects=True
        ),
        cost_estimate=pl.CostEstimate(flops=2**31, bytes_accessed=2**20, transcendentals=2**23),
    )(points, lengthscale.reshape(1, 32), noise, solution, residual, direction)


def solution(mesh):
    in_specs = (P(None, "blk"), P(), P(), P("rep", "blk"), P("rep", "blk"), P("rep", "blk"))
    out_specs = (P("rep", "blk"), P("rep", "blk"), P("rep", "blk"))
    return jax.shard_map(
        on_device, mesh=mesh, in_specs=in_specs, out_specs=out_specs, check_vma=False
    )
```

time: 503 us -> 43.3 us (0.09)
  blocking collectives: 316 us -> 0 us
  matrix products: 125 us -> 0 us
  Pallas kernels: 0 us -> 38.9 us
  loops' own time: 21.5 us -> 0 us
  local copies, waits for them, and re-layouts: 19.1 us -> 2.66 us
  between operations: 14.7 us -> 1.3 us
    all_gather x2 -> x0, blocking collectives: 160 us -> none  [the longest x1 83 us: on_device(): lax.all_gather(sq_norms.astype(jnp.bfloat16), 'blk', axis=1, tiled=True)]
    psum x2 -> x0, blocking collectives: 156 us -> none  [the longest x1 78.9 us: on_device(): lax.psum((jnp.sum(residual * residual, axis=1), jnp.sum(direction * image...]
    dot_general x32 -> x0, matrix products: 125 us -> none  [forward_term(): lax.dot_general(col_dirs, kernel, (((1,), (1,)), ((), ())), preferred_ele...]
    pallas_call x0 -> x1, Pallas kernels: none -> 38.9 us  [on_device(): pl.pallas_call(kernel, out_shape=[jax.ShapeDtypeStruct(direction.shape, f...]
    another operation x1 -> x0, loops' own time: 21.5 us -> none  [on_device(): lax.scan(per_shard, totals, jnp.arange(shards, dtype=jnp.int32))]
    dynamic_slice x64 -> x0, local copies, waits for them, and re-layouts: 19.1 us -> none  [the longest x32 18.8 us: on_device(): lax.scan(per_shard, totals, jnp.arange(shards, dtype=jnp.int32))]
  transfers between devices with their start and end apart: 1 -> 0, of which waited for: 0 -> 0; matrix products, arithmetic and copies ran while one was open for 0% -> 0% of each run, Pallas kernels for 0% -> 0%
where the time goes in v2:
time: 43.3 us; the launch traced here: 42.8 us
  Pallas kernels  38.9 us (90%)
  local copies, waits for them, and re-layouts  2.66 us (6%)
  between operations  1.3 us (3%)
    pallas_call x1, Pallas kernels, on_device(): pl.pallas_call(kernel, out_shape=[jax.ShapeDtypeStruct(direction.shape, f...  38.9 us
    unnamed x7, local copies, waits for them, and re-layouts  2.66 us

profile of v2, /device:TPU:0, one launch (start us, length us, event | category | flops | bytes accessed | tf_op | source)
XLA Modules:
  0.0 42.8 jit_solution(13453672496921150854)
XLA Ops:
  1.3 38.9 %shard_map.85 = (f32[4,1024]{1,0:T(4,128)}, f32[4,1024]{1,0:T(4,128)}, f32[4,1024]{1,0:T(4,128)}) custom-call(f32[32,1024]{1,0:T(8,128)} %points_hbm.1, f32[1,32]{1,0:T(1,128)} %bitcast.1, f32[1]{0:T(128)S(6)} %copy.12.noise_hbm, f32[4,1024]{1,0:T(4,128)} %sol_hbm.1, f32[4,1024]{1,0:T(4,128)} %res_hbm.1, f32[4,1024]{1,0:T(4,128)} %dir_hbm.1), custom_call_target="tpu_custom_call" | custom-call | flops 2147483648 | bytes 1048576 | tf_op jit(solution)/shard_map/pallas_call | solution.py:392
  40.2 0.0 copy-start.1
  40.2 1.3 %copy.13 = f32[4,1024]{1,0:T(4,128)} copy(f32[4,1024]{1,0:T(4,128)} %get-tuple-element.6) | data formatting | bytes 32768
  41.5 0.0 copy-done.1
  41.5 0.0 copy-start
  41.5 0.6 %copy.14 = f32[4,1024]{1,0:T(4,128)} copy(f32[4,1024]{1,0:T(4,128)S(1)} %copy-done.1) | data formatting | bytes 32768
  42.1 0.1 copy-done
  42.2 0.6 %copy.15 = f32[4,1024]{1,0:T(4,128)} copy(f32[4,1024]{1,0:T(4,128)S(1)} %copy-done) | data formatting | bytes 32768
Async XLA Ops:
  40.2 1.3 %copy-start.1 = (f32[4,1024]{1,0:T(4,128)S(1)}, f32[4,1024]{1,0:T(4,128)}, u32[]{:S(2)}) copy-start(f32[4,1024]{1,0:T(4,128)} %get-tuple-element.7) | copy-start | bytes 49156
  41.5 0.7 %copy-start = (f32[4,1024]{1,0:T(4,128)S(1)}, f32[4,1024]{1,0:T(4,128)}, u32[]{:S(2)}) copy-start(f32[4,1024]{1,0:T(4,128)} %get-tuple-element.8) | copy-start | bytes 49156

commit v3 on v2

--- a/solution.py
+++ b/solution.py
@@ -65,6 +65,55 @@
     mine, mydir, pts, dirs, dmat, amat, even, odd, first, second, parts, got, sums,
     load, pts_send, pts_recv, dir_send, dir_recv, part_send, part_recv, sum_send, sum_recv,
 ):
+    blk = lax.axis_index("blk")
+    rep = lax.axis_index("rep")
+    ylo = blk & 1
+    col = blk >> 1
+    x = col >> 2
+    z = col & 3
+    me = ylo * 4 + rep
+
+    def column(dx, dz):
+        return ((x + dx + 4) & 3) * 4 + ((z + dz + 4) & 3)
+
+    def member(c, k):
+        return (c * 2 + (k >> 2), k & 3)
+
+    def slot_column(s):
+        offsets = [SLOTS[m][s] or (0, 0) for m in range(8)]
+        return column(pick(me, [d[0] for d in offsets]), pick(me, [d[1] for d in offsets]))
+
+    slot_cols = [slot_column(s) for s in range(4)]
+    slot_use = [pick(me, [use_of(m, s) for m in range(8)]) for s in range(4)]
+    own_pair = jnp.logical_or(jnp.logical_or(me == 0, me == 1), me == 6)
+    users = [member(column(-dx, -dz), m) for m, s, dx, dz in USES]
+    peers = [((blk + m) & 31, rep) for m in range(1, 32)]
+
+    barrier = pltpu.get_barrier_semaphore()
+
+    def hail(device):
+        pl.semaphore_signal(barrier, inc=1, device_id=device, device_id_type=MESH)
+
+    def if_slot(s, action):
+        if s == 0:
+            action()
+        elif s == 1:
+            pl.when(me != 6)(action)
+        else:
+            pl.when(me >= 6)(action)
+
+    def hail_sources(s):
+        def action():
+            for m in range(1, 8):
+                hail(member(slot_cols[s], (me + m) & 7))
+            if s == 0:
+                pl.when(jnp.logical_not(own_pair))(lambda: hail(member(slot_cols[s], me)))
+            else:
+                hail(member(slot_cols[s], me))
+        return action
+
+    for s in range(4):
+        if_slot(s, hail_sources(s))
     loads = [
         pltpu.make_async_copy(a, b, load.at[n])
         for n, (a, b) in enumerate(
@@ -77,65 +126,6 @@
     for copy in loads:
         copy.start()
 
-    blk = lax.axis_index("blk")
-    rep = lax.axis_index("rep")
-    ylo = blk % 2
-    col = blk // 2
-    x = col // 4
-    z = col % 4
-    me = ylo * 4 + rep
-
-    def column(dx, dz):
-        return ((x + dx + 4) % 4) * 4 + (z + dz + 4) % 4
-
-    def member(c, k):
-        return (c * 2 + k // 4, k % 4)
-
-    def slot_column(s):
-        offsets = [SLOTS[m][s] or (0, 0) for m in range(8)]
-        return column(pick(me, [d[0] for d in offsets]), pick(me, [d[1] for d in offsets]))
-
-    slot_cols = [slot_column(s) for s in range(4)]
-    slot_use = [pick(me, [use_of(m, s) for m in range(8)]) for s in range(4)]
-    own_pair = jnp.logical_or(jnp.logical_or(me == 0, me == 1), me == 6)
-    users = [member(column(-dx, -dz), m) for m, s, dx, dz in USES]
-    peers = [((blk + m) % 32, rep) for m in range(1, 32)]
-
-    barrier = pltpu.get_barrier_semaphore()
-
-    def hail(device):
-        pl.semaphore_signal(barrier, inc=1, device_id=device, device_id_type=MESH)
-
-    def if_slot(s, action):
-        if s == 0:
-            action()
-        elif s == 1:
-            pl.when(me != 6)(action)
-        else:
-            pl.when(me >= 6)(action)
-
-    def hail_sources(s):
-        def action():
-            for k in range(8):
-                if s == 0:
-                    @pl.when(jnp.logical_not(jnp.logical_and(own_pair, me == k)))
-                    def _():
-                        hail(member(slot_cols[s], k))
-                else:
-                    hail(member(slot_cols[s], k))
-        return action
-
-    for s in range(4):
-        if_slot(s, hail_sources(s))
-    for use, device in zip(USES, users):
-        if use[2:] == (0, 0):
-            @pl.when(me != use[0])
-            def _():
-                hail(device)
-        else:
-            hail(device)
-    for device in peers:
-        hail(device)
 
     for copy in loads[:3]:
         copy.wait()
@@ -148,8 +138,7 @@
         [direction[:, c * 256 : (c + 1) * 256] for c in range(4)], axis=0
     ).astype(bf16)
 
-    slots_used = jnp.where(me < 6, 2, jnp.where(me == 6, 3, 4))
-    pl.semaphore_wait(barrier, 8 * slots_used + len(USES) + 31 - 2 * jnp.where(own_pair, 1, 0))
+    pl.semaphore_wait(barrier, len(USES) - jnp.where(own_pair, 1, 0))
 
     def remote(src, dst, send_sem, recv_sem, device):
         return pltpu.make_async_remote_copy(
@@ -157,50 +146,47 @@
             device_id=device, device_id_type=MESH,
         )
 
-    def deliver(src, dst, send_sem, recv_sem, device, is_self, start):
+    def deliver(src, dst, send_sem, recv_sem, device, is_self):
         def away():
-            copy = remote(src, dst, send_sem, recv_sem, device)
-            copy.start() if start else copy.wait_send()
-
-        def here():
-            if start:
-                pltpu.make_async_copy(src, dst, recv_sem).start()
+            remote(src, dst, send_sem, recv_sem, device).start()
 
         if is_self is None:
             away()
         else:
-            pl.when(is_self)(here)
+            pl.when(is_self)(lambda: pltpu.make_async_copy(src, dst, recv_sem).start())
             pl.when(jnp.logical_not(is_self))(away)
 
-    def points_out(start):
-        for r in range(4):
-            @pl.when(rep == r)
-            def _():
-                index = 0
-                for u, (m, s, dx, dz) in enumerate(USES):
-                    if m % 4 == r:
-                        place = s * 2 + ylo
-                        deliver(
-                            mine, pts.at[place, pl.ds(0, 32)], pts_send.at[index], pts_recv.at[place], users[u],
-                            me == m if (dx, dz) == (0, 0) else None, start,
-                        )
-                        index += 1
-
-    def dirs_out(start):
-        for u, (m, s, dx, dz) in enumerate(USES):
-            place = s * 8 + me
-            deliver(
-                mydir, dirs.at[place], dir_send.at[u], dir_recv.at[place], users[u],
-                me == m if (dx, dz) == (0, 0) else None, start,
-            )
-
-    points_out(True)
-    dirs_out(True)
+    def drain(ref, sem):
+        pltpu.make_async_copy(ref, ref, sem).wait()
+
+    def drain_either(alone, ref, count, sem):
+        pl.when(alone)(lambda: drain(ref.at[pl.ds(0, count - 1)], sem))
+        pl.when(jnp.logical_not(alone))(lambda: drain(ref.at[pl.ds(0, count)], sem))
+
+    for u, (m, s, dx, dz) in enumerate(USES):
+        deliver(
+            mydir, dirs.at[s * 8 + me], dir_send.at[0], dir_recv.at[s], users[u],
+            me == m if (dx, dz) == (0, 0) else None,
+        )
+
+    def points_out(r):
+        def action():
+            for u, (m, s, dx, dz) in enumerate(USES):
+                if m % 4 == r:
+                    place = s * 2 + ylo
+                    deliver(
+                        mine, pts.at[place, pl.ds(0, 32)], pts_send.at[0], pts_recv.at[place], users[u],
+                        me == m if (dx, dz) == (0, 0) else None,
+                    )
+        return action
+
+    for r in range(4):
+        pl.when(rep == r)(points_out(r))
     first[...] = jnp.zeros_like(first)
     second[...] = jnp.zeros_like(second)
 
     def augment(place):
-        pltpu.make_async_copy(pts.at[place, pl.ds(0, 32)], pts.at[place, pl.ds(0, 32)], pts_recv.at[place]).wait()
+        drain(pts.at[place, pl.ds(0, 32)], pts_recv.at[place])
         high, mid, low = squares(pts[place, 0:32, :])
         one = jnp.ones((1, BLOCK), f32)
         extra = jnp.concatenate([high, mid, low, one, one, one, jnp.zeros((10, BLOCK), f32)], axis=0)
@@ -219,7 +205,6 @@
         pieces = []
         for r in range(4):
             k = place * 4 + r
-            pltpu.make_async_copy(dirs.at[k], dirs.at[k], dir_recv.at[k]).wait()
             pieces.append(dirs[k].astype(f32))
         for c in range(4):
             rows = jnp.concatenate([p[c * 4 : c * 4 + 4, :] for p in pieces], axis=0)
@@ -230,12 +215,13 @@
             piece = [whole[r * 4 : r * 4 + 4, c * 256 : (c + 1) * 256] for c in range(4)]
             parts[place * 4 + r] = jnp.concatenate(piece, axis=0).astype(bf16)
 
-    def parts_out(s, start):
+    def parts_out(s):
         def action():
-            for k in range(8):
+            for m in range(8):
+                k = (me + m) & 7
                 deliver(
-                    parts.at[s * 8 + k], got.at[slot_use[s]], part_send.at[s * 8 + k], part_recv.at[slot_use[s]],
-                    member(slot_cols[s], k), jnp.logical_and(own_pair, me == k) if s == 0 else None, start,
+                    parts.at[s * 8 + k], got.at[slot_use[s]], part_send.at[s], part_recv.at[0],
+                    member(slot_cols[s], k), own_pair if s == 0 and m == 0 else None,
                 )
         return action
 
@@ -252,11 +238,13 @@
             for y in range(2):
                 augment(right + y)
 
+        drain(dirs.at[pl.ds(left * 4, 8)], dir_recv.at[ph * 2])
         for y in range(2):
             spread(left + y)
 
         @pl.when(jnp.logical_not(diag))
         def _():
+            drain(dirs.at[pl.ds(right * 4, 8)], dir_recv.at[ph * 2 + 1])
             for y in range(2):
                 spread(right + y)
 
@@ -267,21 +255,21 @@
 
         def tile(t):
             u = t - 8
-            half_i = jnp.where(t < 8, t // 4, 2 * early + u // 4)
-            half_j = jnp.where(t < 8, 4 + t % 4, 4 * early + t % 4)
-            v = t // 2
+            half_i = jnp.where(t < 8, t >> 2, 2 * early + (u >> 2))
+            half_j = jnp.where(t < 8, 4 + (t & 3), 4 * early + (t & 3))
+            v = t >> 1
             w = v - 4
             diag_i = jnp.where(v < 4, v, jnp.where(w < 3, 0, jnp.where(w < 5, 1, 2)))
             diag_j = jnp.where(v < 4, v, jnp.where(w < 3, w + 1, jnp.where(w < 5, w - 1, 3)))
-            i = jnp.where(me < 6, t // 8, jnp.where(diag, diag_i, half_i))
-            j = jnp.where(me < 6, t % 8, jnp.where(diag, diag_j * 2 + t % 2, half_j))
+            i = jnp.where(me < 6, t >> 3, jnp.where(diag, diag_i, half_i))
+            j = jnp.where(me < 6, t & 7, jnp.where(diag, diag_j * 2 + (t & 1), half_j))
             return i, j, jnp.logical_and(diag, v < 4)
 
         def place(t):
             i, j, same = tile(t)
-            i0 = pl.multiple_of((i % 2) * ROWS, ROWS)
-            j0 = pl.multiple_of((j % 4) * COLS, COLS)
-            return i // 2, i0, j // 4, j0, same
+            i0 = pl.multiple_of((i & 1) * ROWS, ROWS)
+            j0 = pl.multiple_of((j & 3) * COLS, COLS)
+            return i >> 1, i0, j >> 2, j0, same
 
         def distances(t, out):
             ib, i0, jb, j0, same = place(jnp.minimum(t, count - 1))
@@ -311,7 +299,7 @@
                 products(t + 1, odd)
             return carry
 
-        lax.fori_loop(0, count // 4, step, 0)
+        lax.fori_loop(0, count >> 2, step, 0)
 
         @pl.when(diag)
         def _():
@@ -327,12 +315,12 @@
         @pl.when(ph == 0)
         def _():
             for s in (0, 1):
-                if_slot(s, parts_out(s, True))
+                if_slot(s, parts_out(s))
 
         @pl.when(ph == 1)
         def _():
             for s in (2, 3):
-                parts_out(s, True)()
+                parts_out(s)()
 
         return carry
 
@@ -343,8 +331,8 @@
     residual = res_ref[...]
 
     total = jnp.zeros((16, 256), f32)
+    drain(got, part_recv.at[0])
     for u in range(len(USES)):
-        pltpu.make_async_copy(got.at[u], got.at[u], part_recv.at[u]).wait()
         total += got[u].astype(f32)
     product = jnp.concatenate([total[c * 4 : c * 4 + 4, :] for c in range(4)], axis=1)
     image = 3.0 * product + noise_ref[0] * direction
@@ -360,13 +348,11 @@
     lane = lax.broadcasted_iota(jnp.int32, (16, 128), 1)
     sums[blk] = jnp.sum(jnp.where(row == lane, stats, 0.0), axis=0, keepdims=True)
     copies = [
-        remote(sums.at[blk], sums.at[blk], sum_send.at[m], sum_recv.at[blk], peers[m]) for m in range(31)
+        remote(sums.at[blk], sums.at[blk], sum_send.at[0], sum_recv.at[0], peers[m]) for m in range(31)
     ]
     for copy in copies:
         copy.start()
-    for m in range(1, 32):
-        k = (blk + m) % 32
-        pltpu.make_async_copy(sums.at[k], sums.at[k], sum_recv.at[k]).wait()
+    drain(sums.at[pl.ds(0, 31)], sum_recv.at[0])
     stats = jnp.sum(jnp.where(row == lane, jnp.sum(sums[...], axis=0), 0.0), axis=1, keepdims=True)
     rr, curv, cross, norm = stats[0:4], stats[4:8], stats[8:12], stats[12:16]
     alpha = rr / curv
@@ -376,12 +362,31 @@
     out_res[...] = new_res
     out_dir[...] = new_res + (rr_new / rr) * direction
 
-    points_out(False)
-    dirs_out(False)
+    drain_either(own_pair, dirs, len(USES), dir_send.at[0])
+    for r in range(4):
+        count = sum(m % 4 == r for m, *_ in USES)
+
+        @pl.when(rep == r)
+        def _():
+            drain_either(own_pair, pts.at[:, pl.ds(0, 32)], count, pts_send.at[0])
+
     for s in range(4):
-        if_slot(s, parts_out(s, False))
+        if s == 0:
+            drain_either(own_pair, parts, 8, part_send.at[s])
+        else:
+            if_slot(s, lambda: drain(parts.at[pl.ds(0, 8)], part_send.at[s]))
+    drain(sums.at[pl.ds(0, 31)], sum_send.at[0])
+
+
+def store(a, b, c, out_a, out_b, out_c, sem):
+    copies = [
+        pltpu.make_async_copy(src, dst, sem.at[n])
+        for n, (src, dst) in enumerate([(a, out_a), (b, out_b), (c, out_c)])
+    ]
     for copy in copies:
-        copy.wait_send()
+        copy.start()
+    for copy in copies:
+        copy.wait()
 
 
 def on_device(points, lengthscale, noise, solution, residual, direction):
@@ -389,7 +394,7 @@
     hbm = pl.BlockSpec(memory_space=pltpu.HBM)
     dma = pltpu.SemaphoreType.DMA
     probes = direction.shape[0]
-    return pl.pallas_call(
+    results = pl.pallas_call(
         kernel,
         out_shape=[jax.ShapeDtypeStruct(direction.shape, f32)] * 3,
         in_specs=[hbm] * 6,
@@ -414,14 +419,20 @@
             pltpu.VMEM((32, 16, 256), bf16),
             pltpu.VMEM((len(USES), 16, 256), bf16),
             pltpu.VMEM((32, 1, 128), f32),
-            dma((6,)), dma((6,)), dma((8,)), dma((len(USES),)), dma((32,)), dma((32,)), dma((len(USES),)),
-            dma((31,)), dma((32,)),
+            dma((6,)), dma((1,)), dma((8,)), dma((1,)), dma((4,)), dma((4,)), dma((1,)), dma((1,)), dma((1,)),
         ],
         compiler_params=pltpu.CompilerParams(
             collective_id=0, has_side_effects=True
         ),
         cost_estimate=pl.CostEstimate(flops=2**31, bytes_accessed=2**20, transcendentals=2**23),
     )(points, lengthscale.reshape(1, 32), noise, solution, residual, direction)
+    return pl.pallas_call(
+        store,
+        out_shape=[jax.ShapeDtypeStruct(direction.shape, f32)] * 3,
+        in_specs=[vmem] * 3,
+        out_specs=[hbm] * 3,
+        scratch_shapes=[dma((3,))],
+    )(*results)
 
 
 def solution(mesh):

time: 43.3 us -> 39.4 us (0.910)
  local copies, waits for them, and re-layouts: 2.66 us -> 0 us
  Pallas kernels: 38.9 us -> 37.8 us
    unnamed x7 -> x0, local copies, waits for them, and re-layouts: 2.66 us -> none
    pallas_call x1, Pallas kernels: 38.9 us -> 36.4 us  [on_device(): pl.pallas_call(kernel, out_shape=[jax.ShapeDtypeStruct(direction.shape, f...]
    pallas_call x0 -> x1, Pallas kernels: none -> 1.39 us  [on_device(): pl.pallas_call(store, out_shape=[jax.ShapeDtypeStruct(direction.shape, f3...]
where the time goes in v3:
time: 39.4 us; the launch traced here: 39.1 us
  Pallas kernels  37.8 us (96%)
  between operations  1.28 us (3%)
    pallas_call x1, Pallas kernels, on_device(): pl.pallas_call(kernel, out_shape=[jax.ShapeDtypeStruct(direction.shape, f...  36.4 us
    pallas_call x1, Pallas kernels, on_device(): pl.pallas_call(store, out_shape=[jax.ShapeDtypeStruct(direction.shape, f3...  1.39 us

profile of v3, /device:TPU:0, one launch (start us, length us, event | category | flops | bytes accessed | tf_op | source)
XLA Modules:
  0.0 39.1 jit_solution(9851698681075867460)
XLA Ops:
  1.3 36.4 %shard_map.85 = (f32[4,1024]{1,0:T(4,128)}, f32[4,1024]{1,0:T(4,128)}, f32[4,1024]{1,0:T(4,128)}) custom-call(f32[32,1024]{1,0:T(8,128)} %points_hbm.1, f32[1,32]{1,0:T(1,128)} %bitcast.1, f32[1]{0:T(128)S(6)} %copy.9.noise_hbm, f32[4,1024]{1,0:T(4,128)} %sol_hbm.1, f32[4,1024]{1,0:T(4,128)} %res_hbm.1, f32[4,1024]{1,0:T(4,128)} %dir_hbm.1), custom_call_target="tpu_custom_call" | custom-call | flops 2147483648 | bytes 1048576 | tf_op jit(solution)/shard_map/pallas_call | solution.py:397
  37.7 1.4 %shard_map.86 = (f32[4,1024]{1,0:T(4,128)}, f32[4,1024]{1,0:T(4,128)}, f32[4,1024]{1,0:T(4,128)}) custom-call(f32[4,1024]{1,0:T(4,128)} %get-tuple-element.6.a, f32[4,1024]{1,0:T(4,128)} %get-tuple-element.7.b, f32[4,1024]{1,0:T(4,128)} %get-tuple-element.8.c), custom_call_target="tpu_custom_call" | custom-call | tf_op jit(solution)/shard_map/pallas_call | solution.py:429

commit v4 on v3

--- a/solution.py
+++ b/solution.py
@@ -15,15 +15,17 @@
 COLS = 256
 SCALE = math.sqrt(5.0) / 3.0
 SLOTS = (
+    ((0, -1), (1, 1), None, None),
+    ((-1, 0), (1, 1), None, None),
     ((0, 0), (0, 1), None, None),
     ((0, 0), (1, 0), None, None),
+    ((0, 0), None, (-1, -1), (1, 1)),
     ((-1, 0), (0, 1), None, None),
     ((-1, 0), (0, -1), None, None),
-    ((0, -1), (1, 1), None, None),
-    ((-1, 0), (1, 1), None, None),
-    ((0, 0), None, (-1, -1), (1, 1)),
     ((0, -1), (0, 1), (-1, 0), (1, 0)),
 )
+DIAG = 4
+HALVES = 7
 USES = tuple((m, s) + SLOTS[m][s] for m in range(8) for s in range(4) if SLOTS[m][s] is not None)
 
 
@@ -85,7 +87,8 @@
 
     slot_cols = [slot_column(s) for s in range(4)]
     slot_use = [pick(me, [use_of(m, s) for m in range(8)]) for s in range(4)]
-    own_pair = jnp.logical_or(jnp.logical_or(me == 0, me == 1), me == 6)
+    own_pair = jnp.logical_or(jnp.logical_or(me == 2, me == 3), me == DIAG)
+    two = jnp.logical_or(me == DIAG, me == HALVES)
     users = [member(column(-dx, -dz), m) for m, s, dx, dz in USES]
     peers = [((blk + m) & 31, rep) for m in range(1, 32)]
 
@@ -98,9 +101,9 @@
         if s == 0:
             action()
         elif s == 1:
-            pl.when(me != 6)(action)
+            pl.when(me != DIAG)(action)
         else:
-            pl.when(me >= 6)(action)
+            pl.when(two)(action)
 
     def hail_sources(s):
         def action():
@@ -165,7 +168,7 @@
 
     for u, (m, s, dx, dz) in enumerate(USES):
         deliver(
-            mydir, dirs.at[s * 8 + me], dir_send.at[0], dir_recv.at[s], users[u],
+            mydir, dirs.at[s * 8 + me], dir_send.at[0], dir_recv.at[s * 2 + ylo], users[u],
             me == m if (dx, dz) == (0, 0) else None,
         )
 
@@ -202,10 +205,8 @@
         amat[y] = jnp.transpose(whole).astype(bf16)
 
     def spread(place):
-        pieces = []
-        for r in range(4):
-            k = place * 4 + r
-            pieces.append(dirs[k].astype(f32))
+        drain(dirs.at[pl.ds(place * 4, 4)], dir_recv.at[place])
+        pieces = [dirs[place * 4 + r].astype(f32) for r in range(4)]
         for c in range(4):
             rows = jnp.concatenate([p[c * 4 : c * 4 + 4, :] for p in pieces], axis=0)
             dmat[place, :, c * 256 : (c + 1) * 256] = rows.astype(bf16)
@@ -215,18 +216,19 @@
             piece = [whole[r * 4 : r * 4 + 4, c * 256 : (c + 1) * 256] for c in range(4)]
             parts[place * 4 + r] = jnp.concatenate(piece, axis=0).astype(bf16)
 
-    def parts_out(s):
+    def parts_out(s, y):
         def action():
-            for m in range(8):
-                k = (me + m) & 7
+            for m in range(4):
+                r = (me + m) & 3
                 deliver(
-                    parts.at[s * 8 + k], got.at[slot_use[s]], part_send.at[s], part_recv.at[0],
-                    member(slot_cols[s], k), own_pair if s == 0 and m == 0 else None,
+                    parts.at[s * 8 + y * 4 + r], got.at[slot_use[s]], part_send.at[s], part_recv.at[0],
+                    member(slot_cols[s], y * 4 + r),
+                    jnp.logical_and(own_pair, ylo == y) if s == 0 and m == 0 else None,
                 )
         return action
 
     def phase(ph, carry):
-        diag = jnp.logical_and(me == 6, ph == 0)
+        diag = jnp.logical_and(me == DIAG, ph == 0)
         left = ph * 4
         right = jnp.where(diag, 0, ph * 4 + 2)
         for y in range(2):
@@ -238,20 +240,21 @@
             for y in range(2):
                 augment(right + y)
 
-        drain(dirs.at[pl.ds(left * 4, 8)], dir_recv.at[ph * 2])
-        for y in range(2):
-            spread(left + y)
-
-        @pl.when(jnp.logical_not(diag))
-        def _():
-            drain(dirs.at[pl.ds(right * 4, 8)], dir_recv.at[ph * 2 + 1])
-            for y in range(2):
-                spread(right + y)
+        def spread_pair(b):
+            spread(left + b)
+
+            @pl.when(jnp.logical_not(diag))
+            def _():
+                spread(right + b)
+
+        near = 1 - ylo
+        spread_pair(near)
 
         low_col = jnp.where(ph == 0, slot_cols[0], slot_cols[2])
         high_col = jnp.where(ph == 0, slot_cols[1], slot_cols[3])
         early = jnp.where(low_col < high_col, 0, 1)
-        count = jnp.where(me < 6, 32, jnp.where(diag, 20, 16))
+        full = jnp.logical_not(two)
+        count = jnp.where(full, 32, jnp.where(diag, 20, 16))
 
         def tile(t):
             u = t - 8
@@ -261,8 +264,8 @@
             w = v - 4
             diag_i = jnp.where(v < 4, v, jnp.where(w < 3, 0, jnp.where(w < 5, 1, 2)))
             diag_j = jnp.where(v < 4, v, jnp.where(w < 3, w + 1, jnp.where(w < 5, w - 1, 3)))
-            i = jnp.where(me < 6, t >> 3, jnp.where(diag, diag_i, half_i))
-            j = jnp.where(me < 6, t & 7, jnp.where(diag, diag_j * 2 + (t & 1), half_j))
+            i = jnp.where(full, 2 * ((t >> 4) ^ near) + ((t >> 2) & 1), jnp.where(diag, diag_i, half_i))
+            j = jnp.where(full, 4 * (((t >> 3) & 1) ^ near) + (t & 3), jnp.where(diag, diag_j * 2 + (t & 1), half_j))
             return i, j, jnp.logical_and(diag, v < 4)
 
         def place(t):
@@ -299,32 +302,52 @@
                 products(t + 1, odd)
             return carry
 
-        lax.fori_loop(0, count >> 2, step, 0)
-
-        @pl.when(diag)
-        def _():
-            for y in range(2):
-                pack(y, first[y] + second[y])
+        def finish(side, b):
+            slot = ph * 2 + side
+            whole = (first, second)[side][ph * 2 + b]
+            if side == 0:
+                whole = jnp.where(diag, whole + second[ph * 2 + b], whole)
+            pack(slot * 2 + b, whole)
+            for s in (side, 2 + side):
+                pl.when(ph * 2 + side == s)(parts_out(s, b))
+
+        def segment(q, carry):
+            begin = jnp.where(full, 2 * q, 0)
+            end = jnp.where(full, 2 * q + 2, jnp.where(q == 1, count >> 2, 0))
+            lax.fori_loop(begin, end, step, 0)
+
+            @pl.when(q == 0)
+            def _():
+                spread_pair(ylo)
+
+            @pl.when(jnp.logical_and(full, q == 1))
+            def _():
+                finish(0, near)
+
+            @pl.when(jnp.logical_and(full, q == 2))
+            def _():
+                finish(1, near)
+
+            return carry
+
+        lax.fori_loop(0, 4, segment, 0)
+        finish(0, ylo)
 
         @pl.when(jnp.logical_not(diag))
         def _():
-            for y in range(2):
-                pack(left + y, first[ph * 2 + y])
-                pack(right + y, second[ph * 2 + y])
-
-        @pl.when(ph == 0)
+            finish(1, ylo)
+
+        @pl.when(two)
         def _():
-            for s in (0, 1):
-                if_slot(s, parts_out(s))
-
-        @pl.when(ph == 1)
+            finish(0, near)
+
+        @pl.when(jnp.logical_and(two, jnp.logical_not(diag)))
         def _():
-            for s in (2, 3):
-                parts_out(s)()
+            finish(1, near)
 
         return carry
 
-    lax.fori_loop(0, jnp.where(me < 6, 1, 2), phase, 0)
+    lax.fori_loop(0, jnp.where(two, 2, 1), phase, 0)
 
     for copy in loads[3:]:
         copy.wait()
@@ -419,7 +442,7 @@
             pltpu.VMEM((32, 16, 256), bf16),
             pltpu.VMEM((len(USES), 16, 256), bf16),
             pltpu.VMEM((32, 1, 128), f32),
-            dma((6,)), dma((1,)), dma((8,)), dma((1,)), dma((4,)), dma((4,)), dma((1,)), dma((1,)), dma((1,)),
+            dma((6,)), dma((1,)), dma((8,)), dma((1,)), dma((8,)), dma((4,)), dma((1,)), dma((1,)), dma((1,)),
         ],
         compiler_params=pltpu.CompilerParams(
             collective_id=0, has_side_effects=True

time: 39.4 us -> 37.8 us (0.959)
  Pallas kernels: 37.8 us -> 36.1 us
    pallas_call x1, Pallas kernels: 36.4 us -> 34.7 us  [on_device(): pl.pallas_call(kernel, out_shape=[jax.ShapeDtypeStruct(direction.shape, f...]
where the time goes in v4:
time: 37.8 us; the launch traced here: 37.4 us
  Pallas kernels  36.1 us (96%)
  between operations  1.28 us (3%)
    pallas_call x1, Pallas kernels, on_device(): pl.pallas_call(kernel, out_shape=[jax.ShapeDtypeStruct(direction.shape, f...  34.7 us
    pallas_call x1, Pallas kernels, on_device(): pl.pallas_call(store, out_shape=[jax.ShapeDtypeStruct(direction.shape, f3...  1.39 us

profile of v4, /device:TPU:0, one launch (start us, length us, event | category | flops | bytes accessed | tf_op | source)
XLA Modules:
  0.0 37.4 jit_solution(7124645990977695897)
XLA Ops:
  1.3 34.7 %shard_map.85 = (f32[4,1024]{1,0:T(4,128)}, f32[4,1024]{1,0:T(4,128)}, f32[4,1024]{1,0:T(4,128)}) custom-call(f32[32,1024]{1,0:T(8,128)} %points_hbm.1, f32[1,32]{1,0:T(1,128)} %bitcast.1, f32[1]{0:T(128)S(6)} %copy.9.noise_hbm, f32[4,1024]{1,0:T(4,128)} %sol_hbm.1, f32[4,1024]{1,0:T(4,128)} %res_hbm.1, f32[4,1024]{1,0:T(4,128)} %dir_hbm.1), custom_call_target="tpu_custom_call" | custom-call | flops 2147483648 | bytes 1048576 | tf_op jit(solution)/shard_map/pallas_call | solution.py:420
  36.0 1.4 %shard_map.86 = (f32[4,1024]{1,0:T(4,128)}, f32[4,1024]{1,0:T(4,128)}, f32[4,1024]{1,0:T(4,128)}) custom-call(f32[4,1024]{1,0:T(4,128)} %get-tuple-element.6.a, f32[4,1024]{1,0:T(4,128)} %get-tuple-element.7.b, f32[4,1024]{1,0:T(4,128)} %get-tuple-element.8.c), custom_call_target="tpu_custom_call" | custom-call | tf_op jit(solution)/shard_map/pallas_call | solution.py:452

commit v5 on v4

--- a/solution.py
+++ b/solution.py
@@ -15,18 +15,19 @@
 COLS = 256
 SCALE = math.sqrt(5.0) / 3.0
 SLOTS = (
+    ((-1, -1), (1, 1), (-1, 0), (1, 0)),
+    ((0, 0), (0, 1), None, None),
+    ((0, 0), (1, 0), None, None),
+    ((-1, 0), (0, 1), None, None),
     ((0, -1), (1, 1), None, None),
     ((-1, 0), (1, 1), None, None),
-    ((0, 0), (0, 1), None, None),
-    ((0, 0), (1, 0), None, None),
-    ((0, 0), None, (-1, -1), (1, 1)),
-    ((-1, 0), (0, 1), None, None),
     ((-1, 0), (0, -1), None, None),
     ((0, -1), (0, 1), (-1, 0), (1, 0)),
 )
-DIAG = 4
-HALVES = 7
+OWN = (1, 2)
+HALVES = (0, 7)
 USES = tuple((m, s) + SLOTS[m][s] for m in range(8) for s in range(4) if SLOTS[m][s] is not None)
+URGENT = sorted(range(len(USES)), key=lambda u: (USES[u][1] > 1, -abs(USES[u][2]) - abs(USES[u][3])))
 
 
 def use_of(m, s):
@@ -87,10 +88,12 @@
 
     slot_cols = [slot_column(s) for s in range(4)]
     slot_use = [pick(me, [use_of(m, s) for m in range(8)]) for s in range(4)]
-    own_pair = jnp.logical_or(jnp.logical_or(me == 2, me == 3), me == DIAG)
-    two = jnp.logical_or(me == DIAG, me == HALVES)
+    own_pair = jnp.logical_or(me == OWN[0], me == OWN[1])
+    halves = jnp.logical_or(me == HALVES[0], me == HALVES[1])
     users = [member(column(-dx, -dz), m) for m, s, dx, dz in USES]
-    peers = [((blk + m) & 31, rep) for m in range(1, 32)]
+    hops = (0, 1, 2, 1)
+    masks = sorted(range(1, 32), key=lambda m: -(hops[m >> 3] + hops[(m >> 1) & 3] + (m & 1)))
+    peers = [(blk ^ m, rep) for m in masks]
 
     barrier = pltpu.get_barrier_semaphore()
 
@@ -98,12 +101,10 @@
         pl.semaphore_signal(barrier, inc=1, device_id=device, device_id_type=MESH)
 
     def if_slot(s, action):
-        if s == 0:
+        if s < 2:
             action()
-        elif s == 1:
-            pl.when(me != DIAG)(action)
         else:
-            pl.when(two)(action)
+            pl.when(halves)(action)
 
     def hail_sources(s):
         def action():
@@ -166,16 +167,20 @@
         pl.when(alone)(lambda: drain(ref.at[pl.ds(0, count - 1)], sem))
         pl.when(jnp.logical_not(alone))(lambda: drain(ref.at[pl.ds(0, count)], sem))
 
-    for u, (m, s, dx, dz) in enumerate(USES):
-        deliver(
-            mydir, dirs.at[s * 8 + me], dir_send.at[0], dir_recv.at[s * 2 + ylo], users[u],
-            me == m if (dx, dz) == (0, 0) else None,
-        )
-
-    def points_out(r):
+    def dirs_out(second_pairs):
+        for u in URGENT:
+            m, s, dx, dz = USES[u]
+            if (s > 1) == second_pairs:
+                deliver(
+                    mydir, dirs.at[s * 8 + me], dir_send.at[0], dir_recv.at[s * 2 + ylo], users[u],
+                    me == m if (dx, dz) == (0, 0) else None,
+                )
+
+    def points_out(r, y, second_pairs):
         def action():
-            for u, (m, s, dx, dz) in enumerate(USES):
-                if m % 4 == r:
+            for u in URGENT:
+                m, s, dx, dz = USES[u]
+                if m == y * 4 + r and (s > 1) == second_pairs:
                     place = s * 2 + ylo
                     deliver(
                         mine, pts.at[place, pl.ds(0, 32)], pts_send.at[0], pts_recv.at[place], users[u],
@@ -183,8 +188,16 @@
                     )
         return action
 
+    dirs_out(False)
     for r in range(4):
-        pl.when(rep == r)(points_out(r))
+        for own in range(2):
+            for y in range(2):
+                pl.when(jnp.logical_and(rep == r, ylo == (y if own else 1 - y)))(points_out(r, y, False))
+    dirs_out(True)
+    for r in range(4):
+        for y in range(2):
+            if any(m == y * 4 + r and s > 1 for m, s, *_ in USES):
+                pl.when(rep == r)(points_out(r, y, True))
     first[...] = jnp.zeros_like(first)
     second[...] = jnp.zeros_like(second)
 
@@ -218,8 +231,8 @@
 
     def parts_out(s, y):
         def action():
-            for m in range(4):
-                r = (me + m) & 3
+            for m in (2, 3, 1, 0):
+                r = (me ^ m) & 3
                 deliver(
                     parts.at[s * 8 + y * 4 + r], got.at[slot_use[s]], part_send.at[s], part_recv.at[0],
                     member(slot_cols[s], y * 4 + r),
@@ -228,45 +241,54 @@
         return action
 
     def phase(ph, carry):
-        diag = jnp.logical_and(me == DIAG, ph == 0)
-        left = ph * 4
-        right = jnp.where(diag, 0, ph * 4 + 2)
-        for y in range(2):
-            augment(left + y)
-            left_rows(left + y, y)
-
-        @pl.when(jnp.logical_not(diag))
+        diag = jnp.logical_and(own_pair, ph == 0)
+        full = jnp.logical_not(jnp.logical_or(halves, diag))
+        again = jnp.logical_and(own_pair, ph == 1)
+        left = jnp.where(own_pair, 0, ph * 4)
+        right = jnp.where(own_pair, ph * 2, ph * 4 + 2)
+        near = 1 - ylo
+
+        def left_points(b):
+            @pl.when(jnp.logical_not(again))
+            def _():
+                augment(left + b)
+                left_rows(left + b, b)
+
+        def right_points(b):
+            pl.when(jnp.logical_not(diag))(lambda: augment(right + b))
+
+        def left_dirs(b):
+            pl.when(jnp.logical_not(again))(lambda: spread(left + b))
+
+        def right_dirs(b):
+            pl.when(jnp.logical_not(diag))(lambda: spread(right + b))
+
+        for take in (left_points, right_points, left_dirs, right_dirs):
+            take(near)
+
+        @pl.when(jnp.logical_not(full))
         def _():
-            for y in range(2):
-                augment(right + y)
-
-        def spread_pair(b):
-            spread(left + b)
-
-            @pl.when(jnp.logical_not(diag))
-            def _():
-                spread(right + b)
-
-        near = 1 - ylo
-        spread_pair(near)
+            for take in (left_points, right_points, left_dirs, right_dirs):
+                take(ylo)
 
         low_col = jnp.where(ph == 0, slot_cols[0], slot_cols[2])
         high_col = jnp.where(ph == 0, slot_cols[1], slot_cols[3])
         early = jnp.where(low_col < high_col, 0, 1)
-        full = jnp.logical_not(two)
-        count = jnp.where(full, 32, jnp.where(diag, 20, 16))
+        count = jnp.where(
+            full, 32, jnp.where(diag, jnp.where(me == OWN[0], 8, 12), jnp.where(ph == 0, 16, 8))
+        )
+        skip = jnp.where(jnp.logical_and(me == HALVES[0], ph == 1), 8, 0)
 
         def tile(t):
-            u = t - 8
-            half_i = jnp.where(t < 8, t >> 2, 2 * early + (u >> 2))
-            half_j = jnp.where(t < 8, 4 + (t & 3), 4 * early + (t & 3))
-            v = t >> 1
-            w = v - 4
-            diag_i = jnp.where(v < 4, v, jnp.where(w < 3, 0, jnp.where(w < 5, 1, 2)))
-            diag_j = jnp.where(v < 4, v, jnp.where(w < 3, w + 1, jnp.where(w < 5, w - 1, 3)))
+            h = t + skip
+            half_i = jnp.where(h < 8, h >> 2, 2 * early + ((h >> 2) & 1))
+            half_j = jnp.where(h < 8, 4, 4 * early) + (h & 3)
+            w = t >> 1
+            diag_i = jnp.where(me == OWN[0], w, jnp.where(w < 3, 0, jnp.where(w < 5, 1, 2)))
+            diag_j = jnp.where(me == OWN[0], w, jnp.where(w < 3, w + 1, jnp.where(w < 5, w - 1, 3)))
             i = jnp.where(full, 2 * ((t >> 4) ^ near) + ((t >> 2) & 1), jnp.where(diag, diag_i, half_i))
             j = jnp.where(full, 4 * (((t >> 3) & 1) ^ near) + (t & 3), jnp.where(diag, diag_j * 2 + (t & 1), half_j))
-            return i, j, jnp.logical_and(diag, v < 4)
+            return i, j, jnp.logical_and(diag, me == OWN[0])
 
         def place(t):
             i, j, same = tile(t)
@@ -286,10 +308,10 @@
             weight = jnp.where(same, 0.5, 1.0).astype(bf16)
             di = dmat[left + ib, :, pl.ds(i0, ROWS)] * weight
             dj = dmat[right + jb, :, pl.ds(j0, COLS)] * weight
-            first[ph * 2 + ib, :, pl.ds(i0, ROWS)] += lax.dot_general(
+            first[left + ib, :, pl.ds(i0, ROWS)] += lax.dot_general(
                 dj, values, (((1,), (1,)), ((), ())), preferred_element_type=f32
             )
-            second[ph * 2 + jb, :, pl.ds(j0, COLS)] += jnp.dot(di, values, preferred_element_type=f32)
+            second[right + jb, :, pl.ds(j0, COLS)] += jnp.dot(di, values, preferred_element_type=f32)
 
         distances(0, even)
 
@@ -303,51 +325,40 @@
             return carry
 
         def finish(side, b):
-            slot = ph * 2 + side
-            whole = (first, second)[side][ph * 2 + b]
-            if side == 0:
-                whole = jnp.where(diag, whole + second[ph * 2 + b], whole)
-            pack(slot * 2 + b, whole)
+            slot = (right if side else left) >> 1
+            pack(slot * 2 + b, first[slot * 2 + b] + second[slot * 2 + b])
             for s in (side, 2 + side):
-                pl.when(ph * 2 + side == s)(parts_out(s, b))
+                pl.when(slot == s)(parts_out(s, b))
 
         def segment(q, carry):
-            begin = jnp.where(full, 2 * q, 0)
-            end = jnp.where(full, 2 * q + 2, jnp.where(q == 1, count >> 2, 0))
-            lax.fori_loop(begin, end, step, 0)
-
-            @pl.when(q == 0)
-            def _():
-                spread_pair(ylo)
-
-            @pl.when(jnp.logical_and(full, q == 1))
+            for n, take in ((1, right_points), (2, right_dirs), (3, left_points), (4, left_dirs)):
+                pl.when(jnp.logical_and(full, q == n))(lambda: take(ylo))
+            lax.fori_loop(jnp.where(full, q, 0), jnp.where(full, q + 1, count >> 2), step, 0)
+
+            @pl.when(jnp.logical_and(full, q == 3))
             def _():
                 finish(0, near)
 
-            @pl.when(jnp.logical_and(full, q == 2))
+            @pl.when(jnp.logical_and(full, q == 5))
             def _():
                 finish(1, near)
 
             return carry
 
-        lax.fori_loop(0, 4, segment, 0)
-        finish(0, ylo)
-
+        lax.fori_loop(0, jnp.where(full, 8, 1), segment, 0)
         @pl.when(jnp.logical_not(diag))
         def _():
+            finish(0, ylo)
             finish(1, ylo)
 
-        @pl.when(two)
+        @pl.when(halves)
         def _():
             finish(0, near)
-
-        @pl.when(jnp.logical_and(two, jnp.logical_not(diag)))
-        def _():
             finish(1, near)
 
         return carry
 
-    lax.fori_loop(0, jnp.where(two, 2, 1), phase, 0)
+    lax.fori_loop(0, jnp.where(jnp.logical_or(own_pair, halves), 2, 1), phase, 0)
 
     for copy in loads[3:]:
         copy.wait()
@@ -437,8 +448,8 @@
             pltpu.VMEM((2, BLOCK, 48), bf16),
             pltpu.VMEM((ROWS, COLS), f32),
             pltpu.VMEM((ROWS, COLS), f32),
-            pltpu.VMEM((4, 16, BLOCK), f32),
-            pltpu.VMEM((4, 16, BLOCK), f32),
+            pltpu.VMEM((8, 16, BLOCK), f32),
+            pltpu.VMEM((8, 16, BLOCK), f32),
             pltpu.VMEM((32, 16, 256), bf16),
             pltpu.VMEM((len(USES), 16, 256), bf16),
             pltpu.VMEM((32, 1, 128), f32),

time: 37.8 us -> 36.5 us (0.966)
  Pallas kernels: 36.1 us -> 34.9 us
    pallas_call x1, Pallas kernels: 34.7 us -> 33.5 us  [on_device(): pl.pallas_call(kernel, out_shape=[jax.ShapeDtypeStruct(direction.shape, f...]
where the time goes in v5:
time: 36.5 us; the launch traced here: 36.2 us
  Pallas kernels  34.9 us (96%)
  between operations  1.28 us (4%)
    pallas_call x1, Pallas kernels, on_device(): pl.pallas_call(kernel, out_shape=[jax.ShapeDtypeStruct(direction.shape, f...  33.5 us
    pallas_call x1, Pallas kernels, on_device(): pl.pallas_call(store, out_shape=[jax.ShapeDtypeStruct(direction.shape, f3...  1.39 us

profile of v5, /device:TPU:0, one launch (start us, length us, event | category | flops | bytes accessed | tf_op | source)
XLA Modules:
  0.0 36.2 jit_solution(4702224705766652811)
XLA Ops:
  1.3 33.5 %shard_map.85 = (f32[4,1024]{1,0:T(4,128)}, f32[4,1024]{1,0:T(4,128)}, f32[4,1024]{1,0:T(4,128)}) custom-call(f32[32,1024]{1,0:T(8,128)} %points_hbm.1, f32[1,32]{1,0:T(1,128)} %bitcast.1, f32[1]{0:T(128)S(6)} %copy.9.noise_hbm, f32[4,1024]{1,0:T(4,128)} %sol_hbm.1, f32[4,1024]{1,0:T(4,128)} %res_hbm.1, f32[4,1024]{1,0:T(4,128)} %dir_hbm.1), custom_call_target="tpu_custom_call" | custom-call | flops 2147483648 | bytes 1048576 | tf_op jit(solution)/shard_map/pallas_call | solution.py:431
  34.8 1.4 %shard_map.86 = (f32[4,1024]{1,0:T(4,128)}, f32[4,1024]{1,0:T(4,128)}, f32[4,1024]{1,0:T(4,128)}) custom-call(f32[4,1024]{1,0:T(4,128)} %get-tuple-element.6.a, f32[4,1024]{1,0:T(4,128)} %get-tuple-element.7.b, f32[4,1024]{1,0:T(4,128)} %get-tuple-element.8.c), custom_call_target="tpu_custom_call" | custom-call | tf_op jit(solution)/shard_map/pallas_call | solution.py:463

commit v6 on v5

--- a/solution.py
+++ b/solution.py
@@ -15,16 +15,16 @@
 COLS = 256
 SCALE = math.sqrt(5.0) / 3.0
 SLOTS = (
-    ((-1, -1), (1, 1), (-1, 0), (1, 0)),
+    ((-1, 0), (1, 0), (-1, -1), (1, 1)),
+    ((0, 0), (1, 1), None, None),
     ((0, 0), (0, 1), None, None),
     ((0, 0), (1, 0), None, None),
-    ((-1, 0), (0, 1), None, None),
     ((0, -1), (1, 1), None, None),
+    ((0, 0), (1, -1), None, None),
     ((-1, 0), (1, 1), None, None),
-    ((-1, 0), (0, -1), None, None),
     ((0, -1), (0, 1), (-1, 0), (1, 0)),
 )
-OWN = (1, 2)
+OWN = (2, 3)
 HALVES = (0, 7)
 USES = tuple((m, s) + SLOTS[m][s] for m in range(8) for s in range(4) if SLOTS[m][s] is not None)
 URGENT = sorted(range(len(USES)), key=lambda u: (USES[u][1] > 1, -abs(USES[u][2]) - abs(USES[u][3])))
@@ -89,6 +89,10 @@
     slot_cols = [slot_column(s) for s in range(4)]
     slot_use = [pick(me, [use_of(m, s) for m in range(8)]) for s in range(4)]
     own_pair = jnp.logical_or(me == OWN[0], me == OWN[1])
+    has_own = jnp.bool_(False)
+    for m in range(8):
+        if SLOTS[m][0] == (0, 0):
+            has_own = jnp.logical_or(has_own, me == m)
     halves = jnp.logical_or(me == HALVES[0], me == HALVES[1])
     users = [member(column(-dx, -dz), m) for m, s, dx, dz in USES]
     hops = (0, 1, 2, 1)
@@ -106,18 +110,19 @@
         else:
             pl.when(halves)(action)
 
-    def hail_sources(s):
+    def hail_sources(s, far):
         def action():
-            for m in range(1, 8):
-                hail(member(slot_cols[s], (me + m) & 7))
-            if s == 0:
-                pl.when(jnp.logical_not(own_pair))(lambda: hail(member(slot_cols[s], me)))
-            else:
+            for m in (2, 3) if far else (6, 7, 4, 5, 1):
+                hail(member(slot_cols[s], me ^ m))
+            if not far and s == 0:
+                pl.when(jnp.logical_not(has_own))(lambda: hail(member(slot_cols[s], me)))
+            elif not far:
                 hail(member(slot_cols[s], me))
         return action
 
-    for s in range(4):
-        if_slot(s, hail_sources(s))
+    for far in (True, False):
+        for s in range(4):
+            if_slot(s, hail_sources(s, far))
     loads = [
         pltpu.make_async_copy(a, b, load.at[n])
         for n, (a, b) in enumerate(
@@ -142,7 +147,7 @@
         [direction[:, c * 256 : (c + 1) * 256] for c in range(4)], axis=0
     ).astype(bf16)
 
-    pl.semaphore_wait(barrier, len(USES) - jnp.where(own_pair, 1, 0))
+    pl.semaphore_wait(barrier, len(USES) - jnp.where(has_own, 1, 0))
 
     def remote(src, dst, send_sem, recv_sem, device):
         return pltpu.make_async_remote_copy(
@@ -236,7 +241,7 @@
                 deliver(
                     parts.at[s * 8 + y * 4 + r], got.at[slot_use[s]], part_send.at[s], part_recv.at[0],
                     member(slot_cols[s], y * 4 + r),
-                    jnp.logical_and(own_pair, ylo == y) if s == 0 and m == 0 else None,
+                    jnp.logical_and(has_own, ylo == y) if s == 0 and m == 0 else None,
                 )
         return action
 
@@ -275,9 +280,9 @@
         high_col = jnp.where(ph == 0, slot_cols[1], slot_cols[3])
         early = jnp.where(low_col < high_col, 0, 1)
         count = jnp.where(
-            full, 32, jnp.where(diag, jnp.where(me == OWN[0], 8, 12), jnp.where(ph == 0, 16, 8))
+            full, 32, jnp.where(diag, jnp.where(me == OWN[0], 8, 16), jnp.where((ph == 0) == (me == HALVES[1]), 16, 8))
         )
-        skip = jnp.where(jnp.logical_and(me == HALVES[0], ph == 1), 8, 0)
+        skip = jnp.where(jnp.logical_and(me == HALVES[0], ph == 0), 8, 0)
 
         def tile(t):
             h = t + skip
@@ -305,7 +310,7 @@
         def products(t, dist):
             ib, i0, jb, j0, same = place(t)
             values = matern(dist[...])
-            weight = jnp.where(same, 0.5, 1.0).astype(bf16)
+            weight = jnp.where(same, 0.5, jnp.where(jnp.logical_and(diag, t >= 12), 0.0, 1.0)).astype(bf16)
             di = dmat[left + ib, :, pl.ds(i0, ROWS)] * weight
             dj = dmat[right + jb, :, pl.ds(j0, COLS)] * weight
             first[left + ib, :, pl.ds(i0, ROWS)] += lax.dot_general(
@@ -316,8 +321,8 @@
         distances(0, even)
 
         def step(n, carry):
-            for m in range(2):
-                t = n * 4 + m * 2
+            for m in range(4):
+                t = n * 8 + m * 2
                 distances(t + 1, odd)
                 products(t, even)
                 distances(t + 2, even)
@@ -331,21 +336,21 @@
                 pl.when(slot == s)(parts_out(s, b))
 
         def segment(q, carry):
-            for n, take in ((1, right_points), (2, right_dirs), (3, left_points), (4, left_dirs)):
+            for n, take in ((0, right_points), (1, right_dirs), (1, left_points), (2, left_dirs)):
                 pl.when(jnp.logical_and(full, q == n))(lambda: take(ylo))
-            lax.fori_loop(jnp.where(full, q, 0), jnp.where(full, q + 1, count >> 2), step, 0)
-
-            @pl.when(jnp.logical_and(full, q == 3))
+            lax.fori_loop(jnp.where(full, q, 0), jnp.where(full, q + 1, count >> 3), step, 0)
+
+            @pl.when(jnp.logical_and(full, q == 1))
             def _():
                 finish(0, near)
 
-            @pl.when(jnp.logical_and(full, q == 5))
+            @pl.when(jnp.logical_and(full, q == 2))
             def _():
                 finish(1, near)
 
             return carry
 
-        lax.fori_loop(0, jnp.where(full, 8, 1), segment, 0)
+        lax.fori_loop(0, jnp.where(full, 4, 1), segment, 0)
         @pl.when(jnp.logical_not(diag))
         def _():
             finish(0, ylo)
@@ -396,17 +401,17 @@
     out_res[...] = new_res
     out_dir[...] = new_res + (rr_new / rr) * direction
 
-    drain_either(own_pair, dirs, len(USES), dir_send.at[0])
+    drain_either(has_own, dirs, len(USES), dir_send.at[0])
     for r in range(4):
         count = sum(m % 4 == r for m, *_ in USES)
 
         @pl.when(rep == r)
         def _():
-            drain_either(own_pair, pts.at[:, pl.ds(0, 32)], count, pts_send.at[0])
+            drain_either(has_own, pts.at[:, pl.ds(0, 32)], count, pts_send.at[0])
 
     for s in range(4):
         if s == 0:
-            drain_either(own_pair, parts, 8, part_send.at[s])
+            drain_either(has_own, parts, 8, part_send.at[s])
         else:
             if_slot(s, lambda: drain(parts.at[pl.ds(0, 8)], part_send.at[s]))
     drain(sums.at[pl.ds(0, 31)], sum_send.at[0])

time: 36.5 us -> 35.9 us (0.984)
  Pallas kernels: 34.9 us -> 34.4 us
    pallas_call x1, Pallas kernels: 33.5 us -> 33 us  [on_device(): pl.pallas_call(kernel, out_shape=[jax.ShapeDtypeStruct(direction.shape, f...]
where the time goes in v6:
time: 35.9 us; the launch traced here: 35.7 us
  Pallas kernels  34.4 us (96%)
  between operations  1.28 us (4%)
    pallas_call x1, Pallas kernels, on_device(): pl.pallas_call(kernel, out_shape=[jax.ShapeDtypeStruct(direction.shape, f...  33 us
    pallas_call x1, Pallas kernels, on_device(): pl.pallas_call(store, out_shape=[jax.ShapeDtypeStruct(direction.shape, f3...  1.39 us

profile of v6, /device:TPU:0, one launch (start us, length us, event | category | flops | bytes accessed | tf_op | source)
XLA Modules:
  0.0 35.7 jit_solution(5110885366523968381)
XLA Ops:
  1.3 33.0 %shard_map.85 = (f32[4,1024]{1,0:T(4,128)}, f32[4,1024]{1,0:T(4,128)}, f32[4,1024]{1,0:T(4,128)}) custom-call(f32[32,1024]{1,0:T(8,128)} %points_hbm.1, f32[1,32]{1,0:T(1,128)} %bitcast.1, f32[1]{0:T(128)S(6)} %copy.9.noise_hbm, f32[4,1024]{1,0:T(4,128)} %sol_hbm.1, f32[4,1024]{1,0:T(4,128)} %res_hbm.1, f32[4,1024]{1,0:T(4,128)} %dir_hbm.1), custom_call_target="tpu_custom_call" | custom-call | flops 2147483648 | bytes 1048576 | tf_op jit(solution)/shard_map/pallas_call | solution.py:436
  34.3 1.4 %shard_map.86 = (f32[4,1024]{1,0:T(4,128)}, f32[4,1024]{1,0:T(4,128)}, f32[4,1024]{1,0:T(4,128)}) custom-call(f32[4,1024]{1,0:T(4,128)} %get-tuple-element.6.a, f32[4,1024]{1,0:T(4,128)} %get-tuple-element.7.b, f32[4,1024]{1,0:T(4,128)} %get-tuple-element.8.c), custom_call_target="tpu_custom_call" | custom-call | tf_op jit(solution)/shard_map/pallas_call | solution.py:468

commit v7 on v6

--- a/solution.py
+++ b/solution.py
@@ -1,3 +1,4 @@
+import functools
 import math
 
 import jax
@@ -187,10 +188,14 @@
                 m, s, dx, dz = USES[u]
                 if m == y * 4 + r and (s > 1) == second_pairs:
                     place = s * 2 + ylo
-                    deliver(
-                        mine, pts.at[place, pl.ds(0, 32)], pts_send.at[0], pts_recv.at[place], users[u],
+                    give = functools.partial(
+                        deliver, mine, pts.at[place, pl.ds(0, 32)], pts_send.at[0], pts_recv.at[place], users[u],
                         me == m if (dx, dz) == (0, 0) else None,
                     )
+                    if m == HALVES[1] and s > 1:
+                        pl.when(ylo == s - 2)(give)
+                    else:
+                        give()
         return action
 
     dirs_out(False)
@@ -253,14 +258,17 @@
         right = jnp.where(own_pair, ph * 2, ph * 4 + 2)
         near = 1 - ylo
 
+        quarter = jnp.logical_and(me == HALVES[1], ph == 1)
+
         def left_points(b):
-            @pl.when(jnp.logical_not(again))
+            @pl.when(jnp.logical_not(jnp.logical_or(again, jnp.logical_and(quarter, b == 1))))
             def _():
                 augment(left + b)
                 left_rows(left + b, b)
 
         def right_points(b):
-            pl.when(jnp.logical_not(diag))(lambda: augment(right + b))
+            skipped = jnp.logical_or(diag, jnp.logical_and(quarter, b == 0))
+            pl.when(jnp.logical_not(skipped))(lambda: augment(right + b))
 
         def left_dirs(b):
             pl.when(jnp.logical_not(again))(lambda: spread(left + b))
@@ -369,19 +377,17 @@
         copy.wait()
     residual = res_ref[...]
 
+    own_rr = jnp.sum(residual * residual, axis=1, keepdims=True)
+    shift = noise_ref[0] * direction
     total = jnp.zeros((16, 256), f32)
     drain(got, part_recv.at[0])
     for u in range(len(USES)):
         total += got[u].astype(f32)
     product = jnp.concatenate([total[c * 4 : c * 4 + 4, :] for c in range(4)], axis=1)
-    image = 3.0 * product + noise_ref[0] * direction
+    image = 3.0 * product + shift
 
     stats = jnp.concatenate(
-        [
-            jnp.sum(a, axis=1, keepdims=True)
-            for a in (residual * residual, direction * image, residual * image, image * image)
-        ],
-        axis=0,
+        [own_rr] + [jnp.sum(a * image, axis=1, keepdims=True) for a in (direction, residual, image)], axis=0
     )
     row = lax.broadcasted_iota(jnp.int32, (16, 128), 0)
     lane = lax.broadcasted_iota(jnp.int32, (16, 128), 1)
@@ -403,7 +409,7 @@
 
     drain_either(has_own, dirs, len(USES), dir_send.at[0])
     for r in range(4):
-        count = sum(m % 4 == r for m, *_ in USES)
+        count = sum(m % 4 == r for m, *_ in USES) - (r == HALVES[1] % 4)
 
         @pl.when(rep == r)
         def _():

time: 35.9 us -> 35.9 us (level)
  no operation moved by 1% of the time
where the time goes in v7:
time: 35.9 us; the launch traced here: 35.7 us
  Pallas kernels  34.4 us (96%)
  between operations  1.28 us (4%)
    pallas_call x1, Pallas kernels, on_device(): pl.pallas_call(kernel, out_shape=[jax.ShapeDtypeStruct(direction.shape, f...  33 us
    pallas_call x1, Pallas kernels, on_device(): pl.pallas_call(store, out_shape=[jax.ShapeDtypeStruct(direction.shape, f3...  1.39 us

profile of v7, /device:TPU:0, one launch (start us, length us, event | category | flops | bytes accessed | tf_op | source)
XLA Modules:
  0.0 35.7 jit_solution(13640453261216582569)
XLA Ops:
  1.3 33.0 %shard_map.85 = (f32[4,1024]{1,0:T(4,128)}, f32[4,1024]{1,0:T(4,128)}, f32[4,1024]{1,0:T(4,128)}) custom-call(f32[32,1024]{1,0:T(8,128)} %points_hbm.1, f32[1,32]{1,0:T(1,128)} %bitcast.1, f32[1]{0:T(128)S(6)} %copy.9.noise_hbm, f32[4,1024]{1,0:T(4,128)} %sol_hbm.1, f32[4,1024]{1,0:T(4,128)} %res_hbm.1, f32[4,1024]{1,0:T(4,128)} %dir_hbm.1), custom_call_target="tpu_custom_call" | custom-call | flops 2147483648 | bytes 1048576 | tf_op jit(solution)/shard_map/pallas_call | solution.py:442
  34.3 1.4 %shard_map.86 = (f32[4,1024]{1,0:T(4,128)}, f32[4,1024]{1,0:T(4,128)}, f32[4,1024]{1,0:T(4,128)}) custom-call(f32[4,1024]{1,0:T(4,128)} %get-tuple-element.6.a, f32[4,1024]{1,0:T(4,128)} %get-tuple-element.7.b, f32[4,1024]{1,0:T(4,128)} %get-tuple-element.8.c), custom_call_target="tpu_custom_call" | custom-call | tf_op jit(solution)/shard_map/pallas_call | solution.py:474
